TPU v7x, 128 devices: a whole 4x4x4 slice. The times are simulated.
128 devices in a mesh: row: 4 (over y_lo, core), ma: 32 (over y_hi, x, z).
Axes of the slice: x: 4, y: 4 (y_hi: 2, y_lo: 2; y = y_hi * 2 + y_lo), z: 4, core: 2. Of those that a mesh axis runs over, the one named last changes fastest.
Arguments:
- coeffs: float32 [2, 2048, 2048], P(None, 'ma', 'row'), may hold values from -6 to 6
- legendre: bfloat16 [2048, 128, 2048], P('ma', None, 'row'), may hold values from -0.0029296875 to 0.0029296875
- alpha_table: float32 [64, 2048], P(None, 'row'), may hold values from -4 to 4
- beta_table: float32 [64, 2048], P(None, 'row'), may hold values from -4 to 4
- radial_weight: float32 [64], replicated, may hold values from 0.1 to 1
- radius_index: int32 [64], replicated, may hold values from 0 to 63
- orders: int32 [2048], replicated, may hold values from 0 to 2047, as said below
- cycle_offset: int32 [128], P('ma'), may hold values from 0 to 1
- cycle_weight: float32 [128], P('ma'), may hold values from 0.5 to 2
Outputs:
- gradient: float32 [2, 2048, 2048], P(None, 'ma', 'row')
Inputs may be any that keep to these rules, and one draw needn't show every extreme that they name: orders names every order 0 to 2047 once. The orders 0 to 2047 fall into blocks of 64 consecutive ones; the 64 slots of each index of ma hold exactly two orders of each block, one of its lower half and its mirror in the upper half.
All inputs are finite; a program needn't handle non-finite values.
Results may differ from a plain program's by a relative error of at most 0.0049.
Values may be sent and summed in bfloat16 or wider, within the bound.
A program may use at most 192 MiB of HBM per device.

v0:
```python
import math

import jax
import jax.numpy as jnp
from jax import lax
from jax.sharding import PartitionSpec as P

NPIX = 4096


def synth_rows(row_count, coeff_rows, alpha_table, beta_table, radius_index, legendre):
    filters = jnp.stack([alpha_table[radius_index], beta_table[radius_index]], axis=1)
    local_orders = coeff_rows.shape[0]
    local_degrees = coeff_rows.shape[2]
    cycle_count = legendre.shape[1]
    filtered = (filters[None, :, :, None, :] * coeff_rows[:, None, None, :, :]).astype(jnp.bfloat16)
    filtered = filtered.reshape(local_orders, row_count * 4, local_degrees)
    harmonic = lax.dot_general(
        filtered, legendre, (((2,), (2,)), ((0,), (0,))), preferred_element_type=jnp.float32
    )
    harmonic = harmonic.reshape(local_orders, row_count, 2, 2, cycle_count)
    return jnp.transpose(harmonic, (1, 4, 2, 0, 3)).reshape(
        row_count, cycle_count, 2, 2 * local_orders
    )


def cycle_work(shard_piece, orders, cycle_offset, cycle_weight):
    row_count = shard_piece.shape[0]
    cycle_local = shard_piece.shape[1]
    peer_count = shard_piece.shape[3]
    order_count = orders.shape[0]
    row_total = row_count * cycle_local * 2
    rotation = (orders[None, :] * cycle_offset[:, None]).astype(jnp.float32) * (math.pi / NPIX)
    cos_turn = jnp.cos(rotation)[None, :, None, :]
    sin_turn = jnp.sin(rotation)[None, :, None, :]
    separated = shard_piece.reshape(row_count, cycle_local, 2, order_count, 2)
    real_part = separated[..., 0]
    imag_part = separated[..., 1]
    doubling = jnp.where(orders == 0, 1.0, 2.0).astype(jnp.float32)
    rotated_re = ((cos_turn * real_part - sin_turn * imag_part) * doubling).reshape(
        row_total, order_count
    )
    rotated_im = ((sin_turn * real_part + cos_turn * imag_part) * doubling).reshape(
        row_total, order_count
    )
    block_width = 512
    block_count = NPIX // block_width
    pixel_ids = jnp.arange(block_width, dtype=jnp.int32)

    def block_step(block_id, carry):
        cos_sum, sin_sum, totals = carry
        first_pixel = block_id * block_width + pixel_ids
        phase_index = orders[:, None] * first_pixel[None, :] % NPIX
        angles = phase_index.astype(jnp.float32) * (2.0 * math.pi / NPIX)
        cos_table = jnp.cos(angles)
        sin_table = jnp.sin(angles)
        pixels = jnp.dot(
            rotated_re,
            cos_table,
            precision=lax.Precision.HIGHEST,
            preferred_element_type=jnp.float32,
        )
        pixels = pixels - jnp.dot(
            rotated_im,
            sin_table,
            precision=lax.Precision.HIGHEST,
            preferred_element_type=jnp.float32,
        )
        pixels = pixels.reshape(row_count, cycle_local, 2, block_width)
        field_a = pixels[:, :, 0]
        field_b = pixels[:, :, 1]
        products = jnp.stack([field_b * field_b, field_a * field_b], axis=2).reshape(
            row_total, block_width
        )
        contract = (((1,), (1,)), ((), ()))
        cos_sum = cos_sum + lax.dot_general(
            products,
            cos_table,
            contract,
            precision=lax.Precision.HIGHEST,
            preferred_element_type=jnp.float32,
        )
        sin_sum = sin_sum - lax.dot_general(
            products,
            sin_table,
            contract,
            precision=lax.Precision.HIGHEST,
            preferred_element_type=jnp.float32,
        )
        totals = totals + jnp.sum(products, axis=1)
        return (cos_sum, sin_sum, totals)

    start_spec = jnp.zeros((row_total, order_count), jnp.float32)
    cos_sum, sin_sum, totals = lax.fori_loop(
        0, block_count, block_step, (start_spec, start_spec, jnp.zeros((row_total,), jnp.float32))
    )
    is_zero = (orders == 0).astype(jnp.float32)
    cos_sum = cos_sum - totals[:, None] * is_zero[None, :]
    cos_part = cos_sum.reshape(row_count, cycle_local, 2, order_count)
    sin_part = sin_sum.reshape(row_count, cycle_local, 2, order_count)
    cycle_scale = cycle_weight[None, :, None, None]
    analysed_re = (cos_turn * cos_part + sin_turn * sin_part) * cycle_scale
    analysed_im = (cos_turn * sin_part - sin_turn * cos_part) * cycle_scale
    analysed = jnp.stack([analysed_re, analysed_im], axis=-1)
    analysed = analysed.reshape(
        row_count, cycle_local, 2, peer_count, 2 * order_count // peer_count
    )
    return analysed.astype(jnp.bfloat16)


def adjoint_rows(shard_piece, legendre, alpha_table, beta_table, radial_weight, radius_index):
    local_orders = shard_piece.shape[0]
    row_count = shard_piece.shape[1]
    cycle_count = shard_piece.shape[3]
    local_degrees = legendre.shape[2]
    left_rows = shard_piece.reshape(local_orders, row_count * 4, cycle_count)
    adjoint_terms = lax.dot_general(
        left_rows, legendre, (((2,), (1,)), ((0,), (0,))), preferred_element_type=jnp.float32
    )
    adjoint_terms = adjoint_terms.reshape(local_orders, row_count, 2, 2, local_degrees)
    radial = radial_weight[radius_index][:, None]
    alpha_weighted = (radial * alpha_table[radius_index])[None, :, None, :]
    beta_weighted = (2.0 * radial * beta_table[radius_index])[None, :, None, :]
    return jnp.sum(
        adjoint_terms[:, :, 0] * alpha_weighted + adjoint_terms[:, :, 1] * beta_weighted, axis=1
    )


def body(
    coeffs,
    legendre,
    alpha_table,
    beta_table,
    radial_weight,
    radius_index,
    orders,
    cycle_offset,
    cycle_weight,
):
    row_id = lax.axis_index("row")
    ma_id = lax.axis_index("ma")
    local_orders = coeffs.shape[1]
    local_degrees = coeffs.shape[2]
    cycle_count = legendre.shape[1]
    radius_count = radius_index.shape[0]
    radii_here = radius_count // lax.axis_size("row")
    my_orders = lax.dynamic_slice_in_dim(orders, ma_id * local_orders, local_orders)
    degree = row_id * local_degrees + jnp.arange(local_degrees, dtype=jnp.int32)
    live_mask = (degree[None, :] >= my_orders[:, None]).astype(jnp.float32)
    coeff_rows = jnp.transpose(coeffs * live_mask[None], (1, 0, 2))
    summed = lax.psum(
        synth_rows(radius_count, coeff_rows, alpha_table, beta_table, radius_index, legendre), "row"
    )
    own_fields = lax.dynamic_slice_in_dim(summed, row_id * radii_here, radii_here, 0)
    own_fields = own_fields.reshape(radii_here, cycle_count, 2, 1, 2 * local_orders)
    shard_piece = lax.all_to_all(own_fields, "ma", split_axis=1, concat_axis=3, tiled=True)
    flat_piece = shard_piece.reshape(
        shard_piece.shape[0], shard_piece.shape[1], 2, shard_piece.shape[3] * shard_piece.shape[4]
    )
    analysed = cycle_work(flat_piece, orders, cycle_offset, cycle_weight)
    returned = lax.all_to_all(analysed, "ma", split_axis=3, concat_axis=1, tiled=True)
    returned = returned.reshape(radii_here, cycle_count, 2, local_orders, 2)
    returned = jnp.transpose(returned, (3, 0, 2, 4, 1)).reshape(
        local_orders, radii_here, 4, cycle_count
    )
    gradient = adjoint_rows(
        lax.all_gather(returned, "row", axis=1, tiled=True),
        legendre,
        alpha_table,
        beta_table,
        radial_weight,
        radius_index,
    )
    gradient = gradient * live_mask[:, None, :]
    return jnp.transpose(gradient, (1, 0, 2))


def solution(mesh):
    in_specs = (
        P(None, "ma", "row"),
        P("ma", None, "row"),
        P(None, "row"),
        P(None, "row"),
        P(),
        P(),
        P(),
        P("ma"),
        P("ma"),
    )
    out_specs = P(None, "ma", "row")
    return jax.shard_map(body, mesh=mesh, in_specs=in_specs, out_specs=out_specs, check_vma=False)
```

profile of v0, /device:TPU:15, one launch (start us, length us, event | category | flops | bytes accessed | tf_op | source)
XLA Modules:
  0.0 1277.8 jit_solution(8880597544364554095)
XLA Ops:
  20.4 39.8 %mul.385 = f32[64,256,512]{2,1,0:T(8,128)} reshape(f32[64,64,2,2,512]{4,3,2,1,0:T(2,128)} %mul.384) | data formatting | bytes 67108864 | tf_op jit(solution)/shard_map/mul | solution.py:16
  62.4 20.0 %fusion.36 = f32[64,256,128]{2,1,0:T(8,128)} fusion(bf16[64,128,512]{2,1,0:T(8,128)(2,1)} %param.12, f32[64,256,512]{2,1,0:T(8,128)} %mul.385, f32[256,512]{1,0:T(8,128)S(1)} %mul.378), kind=kOutput, calls=%fused_computation.43 | convolution fusion | flops 2164260864 | bytes 50855936 | tf_op jit(solution)/shard_map/dot_general | solution.py:18
  90.4 160.6 %all-reduce.2.cloned.1.call-done = f32[64,128,2,128]{1,0,3,2:T(8,128)} async-done(((f32[64,128,2,128]{1,0,3,2:T(8,128)}), f32[64,128,2,128]{1,0,3,2:T(8,128)}) %all-reduce.2.cloned.1.call-update) | async-done | bytes 8388624 | tf_op jit(solution)/shard_map/psum | solution.py:151
  268.6 24.3 %all-to-all-done = f32[16,128,2,1,128]{4,3,2,0,1:T(1,128)} async-done(((f32[16,128,2,1,128]{4,3,2,0,1:T(1,128)}), f32[16,128,2,1,128]{4,3,2,0,1:T(1,128)}, u32[]{:S(2)}, u32[]{:S(2)}) %all-to-all-start) | async-done | bytes 2097184 | tf_op jit(solution)/shard_map/all_to_all | solution.py:156
  303.5 19.5 %fusion.46 = (f32[16,4,2,2048,1]{0,4,3,2,1:T(1,128)}, f32[16,4,2,2048,1]{0,4,3,2,1:T(1,128)}) fusion(f32[16,4,2,2048,2]{0,4,3,2,1:T(2,128)} %bitcast.71), kind=kLoop, calls=%fused_computation.75 | loop fusion | bytes 4194304 | tf_op jit(solution)/shard_map/slice | solution.py:37
  323.0 17.4 %copy.100 = f32[16,4,2,2048,1]{3,2,1,0,4:T(2,128)S(1)} copy(f32[16,4,2,2048,1]{0,4,3,2,1:T(1,128)} %get-tuple-element.255) | data formatting | bytes 2097152 | tf_op jit(solution)/shard_map/slice | solution.py:37
  342.2 17.5 %copy.101 = f32[16,4,2,2048,1]{3,2,1,0,4:T(2,128)S(1)} copy(f32[16,4,2,2048,1]{0,4,3,2,1:T(1,128)} %get-tuple-element.256) | data formatting | bytes 2097152 | tf_op jit(solution)/shard_map/slice | solution.py:38
  364.8 653.2 %while.20 = (s32[]{:T(128)}, f32[128,2048]{1,0:T(8,128)}, f32[128,2048]{1,0:T(8,128)}, f32[128]{0:T(128)S(1)}, s32[2048]{0:T(1024)S(1)}, /*index=5*/f32[128,2048...) while((s32[]{:T(128)}, f32[128,2048]{1,0:T(8,128)}, f32[128,2048]{1,0:T(8,128)}, ...), condition=%wide.region_3.4_spmd.clone, body=%wide.region_1.3_spmd.clone.sunk | while | flops 6502482944 | bytes 30717196 | solution.py:94
  365.0 19.2 %fusion.75 = f32[512,128]{0,1:T(8,128)S(1)} fusion(f32[128,2048]{1,0:T(8,128)} %get-tuple-element.341, s32[512]{0:T(512)S(1)} %iota_add_fusion.3, s32[2048]{0:T(1024)S(1)} %get-tuple-element.340), kind=kOutput, calls=%fused_computation.16.clone.1 | convolution fusion | flops 1625292800 | bytes 1320960 | tf_op jit(solution)/shard_map/while/body/eval_jaxpr/dot_general | solution.py:57
  384.2 18.4 %fusion.76 = f32[128,512]{1,0:T(8,128)S(1)} fusion(f32[512,128]{0,1:T(8,128)S(1)} %fusion.75, f32[128,2048]{1,0:T(8,128)S(1)} %copy-done.16, s32[512]{0:T(512)S(1)} %iota_add_fusion.3, s32[2048]{0:T(1024)S(1)} %get-tuple-element.340), kind=kOutput, calls=%fused_computation.19.clone.1 | convolution fusion | flops 1625358336 | bytes 1583104 | tf_op jit(solution)/shard_map/while/body/eval_jaxpr/dot_general | solution.py:63
  403.6 19.2 %convolution_subtract_fusion.2 = f32[128,2048]{1,0:T(8,128)S(1)} fusion(f32[128,512]{1,0:T(8,128)S(1)} %reshape.326, s32[512]{0:T(512)S(1)} %iota_add_fusion.3, s32[2048]{0:T(1024)S(1)} %get-tuple-element.340, f32[128,2048]{1,0:T(8,128)S(1)} %copy-done.13, pred[]{:T(512)S(6)} %compare.4), kind=kOutput, calls=%fused_computation.12.clone.1 | convolution fusion | flops 1625817088 | bytes 2369537 | tf_op jit(solution)/shard_map/while/body/eval_jaxpr/dot_general | solution.py:83
  422.8 19.5 %convolution_add_fusion.2 = f32[128,2048]{1,0:T(8,128)S(1)} fusion(f32[128,512]{1,0:T(8,128)S(1)} %reshape.326, s32[512]{0:T(512)S(1)} %iota_add_fusion.3, s32[2048]{0:T(1024)S(1)} %get-tuple-element.340, f32[128,2048]{1,0:T(8,128)S(1)} %copy-done.11, pred[]{:T(512)S(6)} %compare.4), kind=kOutput, calls=%fused_computation.13.clone.1 | convolution fusion | flops 1625817088 | bytes 2369537 | tf_op jit(solution)/shard_map/while/body/eval_jaxpr/dot_general | solution.py:76
  445.8 19.4 %fusion.75 = f32[512,128]{0,1:T(8,128)S(1)} fusion(f32[128,2048]{1,0:T(8,128)} %get-tuple-element.341, s32[512]{0:T(512)S(1)} %iota_add_fusion.3, s32[2048]{0:T(1024)S(1)} %get-tuple-element.340), kind=kOutput, calls=%fused_computation.16.clone.1 | convolution fusion | flops 1625292800 | bytes 1320960 | tf_op jit(solution)/shard_map/while/body/eval_jaxpr/dot_general | solution.py:57
  465.2 18.2 %fusion.76 = f32[128,512]{1,0:T(8,128)S(1)} fusion(f32[512,128]{0,1:T(8,128)S(1)} %fusion.75, f32[128,2048]{1,0:T(8,128)S(1)} %copy-done.16, s32[512]{0:T(512)S(1)} %iota_add_fusion.3, s32[2048]{0:T(1024)S(1)} %get-tuple-element.340), kind=kOutput, calls=%fused_computation.19.clone.1 | convolution fusion | flops 1625358336 | bytes 1583104 | tf_op jit(solution)/shard_map/while/body/eval_jaxpr/dot_general | solution.py:63
  484.4 19.4 %convolution_subtract_fusion.2 = f32[128,2048]{1,0:T(8,128)S(1)} fusion(f32[128,512]{1,0:T(8,128)S(1)} %reshape.326, s32[512]{0:T(512)S(1)} %iota_add_fusion.3, s32[2048]{0:T(1024)S(1)} %get-tuple-element.340, f32[128,2048]{1,0:T(8,128)S(1)} %copy-done.13, pred[]{:T(512)S(6)} %compare.4), kind=kOutput, calls=%fused_computation.12.clone.1 | convolution fusion | flops 1625817088 | bytes 2369537 | tf_op jit(solution)/shard_map/while/body/eval_jaxpr/dot_general | solution.py:83
  503.8 19.3 %convolution_add_fusion.2 = f32[128,2048]{1,0:T(8,128)S(1)} fusion(f32[128,512]{1,0:T(8,128)S(1)} %reshape.326, s32[512]{0:T(512)S(1)} %iota_add_fusion.3, s32[2048]{0:T(1024)S(1)} %get-tuple-element.340, f32[128,2048]{1,0:T(8,128)S(1)} %copy-done.11, pred[]{:T(512)S(6)} %compare.4), kind=kOutput, calls=%fused_computation.13.clone.1 | convolution fusion | flops 1625817088 | bytes 2369537 | tf_op jit(solution)/shard_map/while/body/eval_jaxpr/dot_general | solution.py:76
  526.8 19.2 %fusion.75 = f32[512,128]{0,1:T(8,128)S(1)} fusion(f32[128,2048]{1,0:T(8,128)} %get-tuple-element.341, s32[512]{0:T(512)S(1)} %iota_add_fusion.3, s32[2048]{0:T(1024)S(1)} %get-tuple-element.340), kind=kOutput, calls=%fused_computation.16.clone.1 | convolution fusion | flops 1625292800 | bytes 1320960 | tf_op jit(solution)/shard_map/while/body/eval_jaxpr/dot_general | solution.py:57
  546.0 18.5 %fusion.76 = f32[128,512]{1,0:T(8,128)S(1)} fusion(f32[512,128]{0,1:T(8,128)S(1)} %fusion.75, f32[128,2048]{1,0:T(8,128)S(1)} %copy-done.16, s32[512]{0:T(512)S(1)} %iota_add_fusion.3, s32[2048]{0:T(1024)S(1)} %get-tuple-element.340), kind=kOutput, calls=%fused_computation.19.clone.1 | convolution fusion | flops 1625358336 | bytes 1583104 | tf_op jit(solution)/shard_map/while/body/eval_jaxpr/dot_general | solution.py:63
  565.4 19.2 %convolution_subtract_fusion.2 = f32[128,2048]{1,0:T(8,128)S(1)} fusion(f32[128,512]{1,0:T(8,128)S(1)} %reshape.326, s32[512]{0:T(512)S(1)} %iota_add_fusion.3, s32[2048]{0:T(1024)S(1)} %get-tuple-element.340, f32[128,2048]{1,0:T(8,128)S(1)} %copy-done.13, pred[]{:T(512)S(6)} %compare.4), kind=kOutput, calls=%fused_computation.12.clone.1 | convolution fusion | flops 1625817088 | bytes 2369537 | tf_op jit(solution)/shard_map/while/body/eval_jaxpr/dot_general | solution.py:83
  584.6 19.5 %convolution_add_fusion.2 = f32[128,2048]{1,0:T(8,128)S(1)} fusion(f32[128,512]{1,0:T(8,128)S(1)} %reshape.326, s32[512]{0:T(512)S(1)} %iota_add_fusion.3, s32[2048]{0:T(1024)S(1)} %get-tuple-element.340, f32[128,2048]{1,0:T(8,128)S(1)} %copy-done.11, pred[]{:T(512)S(6)} %compare.4), kind=kOutput, calls=%fused_computation.13.clone.1 | convolution fusion | flops 1625817088 | bytes 2369537 | tf_op jit(solution)/shard_map/while/body/eval_jaxpr/dot_general | solution.py:76
  607.5 19.2 %fusion.75 = f32[512,128]{0,1:T(8,128)S(1)} fusion(f32[128,2048]{1,0:T(8,128)} %get-tuple-element.341, s32[512]{0:T(512)S(1)} %iota_add_fusion.3, s32[2048]{0:T(1024)S(1)} %get-tuple-element.340), kind=kOutput, calls=%fused_computation.16.clone.1 | convolution fusion | flops 1625292800 | bytes 1320960 | tf_op jit(solution)/shard_map/while/body/eval_jaxpr/dot_general | solution.py:57
  626.8 18.4 %fusion.76 = f32[128,512]{1,0:T(8,128)S(1)} fusion(f32[512,128]{0,1:T(8,128)S(1)} %fusion.75, f32[128,2048]{1,0:T(8,128)S(1)} %copy-done.16, s32[512]{0:T(512)S(1)} %iota_add_fusion.3, s32[2048]{0:T(1024)S(1)} %get-tuple-element.340), kind=kOutput, calls=%fused_computation.19.clone.1 | convolution fusion | flops 1625358336 | bytes 1583104 | tf_op jit(solution)/shard_map/while/body/eval_jaxpr/dot_general | solution.py:63
  646.1 19.2 %convolution_subtract_fusion.2 = f32[128,2048]{1,0:T(8,128)S(1)} fusion(f32[128,512]{1,0:T(8,128)S(1)} %reshape.326, s32[512]{0:T(512)S(1)} %iota_add_fusion.3, s32[2048]{0:T(1024)S(1)} %get-tuple-element.340, f32[128,2048]{1,0:T(8,128)S(1)} %copy-done.13, pred[]{:T(512)S(6)} %compare.4), kind=kOutput, calls=%fused_computation.12.clone.1 | convolution fusion | flops 1625817088 | bytes 2369537 | tf_op jit(solution)/shard_map/while/body/eval_jaxpr/dot_general | solution.py:83
  665.4 19.5 %convolution_add_fusion.2 = f32[128,2048]{1,0:T(8,128)S(1)} fusion(f32[128,512]{1,0:T(8,128)S(1)} %reshape.326, s32[512]{0:T(512)S(1)} %iota_add_fusion.3, s32[2048]{0:T(1024)S(1)} %get-tuple-element.340, f32[128,2048]{1,0:T(8,128)S(1)} %copy-done.11, pred[]{:T(512)S(6)} %compare.4), kind=kOutput, calls=%fused_computation.13.clone.1 | convolution fusion | flops 1625817088 | bytes 2369537 | tf_op jit(solution)/shard_map/while/body/eval_jaxpr/dot_general | solution.py:76
  688.3 19.4 %fusion.75 = f32[512,128]{0,1:T(8,128)S(1)} fusion(f32[128,2048]{1,0:T(8,128)} %get-tuple-element.341, s32[512]{0:T(512)S(1)} %iota_add_fusion.3, s32[2048]{0:T(1024)S(1)} %get-tuple-element.340), kind=kOutput, calls=%fused_computation.16.clone.1 | convolution fusion | flops 1625292800 | bytes 1320960 | tf_op jit(solution)/shard_map/while/body/eval_jaxpr/dot_general | solution.py:57
  707.8 18.2 %fusion.76 = f32[128,512]{1,0:T(8,128)S(1)} fusion(f32[512,128]{0,1:T(8,128)S(1)} %fusion.75, f32[128,2048]{1,0:T(8,128)S(1)} %copy-done.16, s32[512]{0:T(512)S(1)} %iota_add_fusion.3, s32[2048]{0:T(1024)S(1)} %get-tuple-element.340), kind=kOutput, calls=%fused_computation.19.clone.1 | convolution fusion | flops 1625358336 | bytes 1583104 | tf_op jit(solution)/shard_map/while/body/eval_jaxpr/dot_general | solution.py:63
  726.9 19.4 %convolution_subtract_fusion.2 = f32[128,2048]{1,0:T(8,128)S(1)} fusion(f32[128,512]{1,0:T(8,128)S(1)} %reshape.326, s32[512]{0:T(512)S(1)} %iota_add_fusion.3, s32[2048]{0:T(1024)S(1)} %get-tuple-element.340, f32[128,2048]{1,0:T(8,128)S(1)} %copy-done.13, pred[]{:T(512)S(6)} %compare.4), kind=kOutput, calls=%fused_computation.12.clone.1 | convolution fusion | flops 1625817088 | bytes 2369537 | tf_op jit(solution)/shard_map/while/body/eval_jaxpr/dot_general | solution.py:83
  746.4 19.3 %convolution_add_fusion.2 = f32[128,2048]{1,0:T(8,128)S(1)} fusion(f32[128,512]{1,0:T(8,128)S(1)} %reshape.326, s32[512]{0:T(512)S(1)} %iota_add_fusion.3, s32[2048]{0:T(1024)S(1)} %get-tuple-element.340, f32[128,2048]{1,0:T(8,128)S(1)} %copy-done.11, pred[]{:T(512)S(6)} %compare.4), kind=kOutput, calls=%fused_computation.13.clone.1 | convolution fusion | flops 1625817088 | bytes 2369537 | tf_op jit(solution)/shard_map/while/body/eval_jaxpr/dot_general | solution.py:76
  769.3 19.2 %fusion.75 = f32[512,128]{0,1:T(8,128)S(1)} fusion(f32[128,2048]{1,0:T(8,128)} %get-tuple-element.341, s32[512]{0:T(512)S(1)} %iota_add_fusion.3, s32[2048]{0:T(1024)S(1)} %get-tuple-element.340), kind=kOutput, calls=%fused_computation.16.clone.1 | convolution fusion | flops 1625292800 | bytes 1320960 | tf_op jit(solution)/shard_map/while/body/eval_jaxpr/dot_general | solution.py:57
  788.6 18.5 %fusion.76 = f32[128,512]{1,0:T(8,128)S(1)} fusion(f32[512,128]{0,1:T(8,128)S(1)} %fusion.75, f32[128,2048]{1,0:T(8,128)S(1)} %copy-done.16, s32[512]{0:T(512)S(1)} %iota_add_fusion.3, s32[2048]{0:T(1024)S(1)} %get-tuple-element.340), kind=kOutput, calls=%fused_computation.19.clone.1 | convolution fusion | flops 1625358336 | bytes 1583104 | tf_op jit(solution)/shard_map/while/body/eval_jaxpr/dot_general | solution.py:63
  807.9 19.2 %convolution_subtract_fusion.2 = f32[128,2048]{1,0:T(8,128)S(1)} fusion(f32[128,512]{1,0:T(8,128)S(1)} %reshape.326, s32[512]{0:T(512)S(1)} %iota_add_fusion.3, s32[2048]{0:T(1024)S(1)} %get-tuple-element.340, f32[128,2048]{1,0:T(8,128)S(1)} %copy-done.13, pred[]{:T(512)S(6)} %compare.4), kind=kOutput, calls=%fused_computation.12.clone.1 | convolution fusion | flops 1625817088 | bytes 2369537 | tf_op jit(solution)/shard_map/while/body/eval_jaxpr/dot_general | solution.py:83
  827.2 19.5 %convolution_add_fusion.2 = f32[128,2048]{1,0:T(8,128)S(1)} fusion(f32[128,512]{1,0:T(8,128)S(1)} %reshape.326, s32[512]{0:T(512)S(1)} %iota_add_fusion.3, s32[2048]{0:T(1024)S(1)} %get-tuple-element.340, f32[128,2048]{1,0:T(8,128)S(1)} %copy-done.11, pred[]{:T(512)S(6)} %compare.4), kind=kOutput, calls=%fused_computation.13.clone.1 | convolution fusion | flops 1625817088 | bytes 2369537 | tf_op jit(solution)/shard_map/while/body/eval_jaxpr/dot_general | solution.py:76
  850.1 19.2 %fusion.75 = f32[512,128]{0,1:T(8,128)S(1)} fusion(f32[128,2048]{1,0:T(8,128)} %get-tuple-element.341, s32[512]{0:T(512)S(1)} %iota_add_fusion.3, s32[2048]{0:T(1024)S(1)} %get-tuple-element.340), kind=kOutput, calls=%fused_computation.16.clone.1 | convolution fusion | flops 1625292800 | bytes 1320960 | tf_op jit(solution)/shard_map/while/body/eval_jaxpr/dot_general | solution.py:57
  869.4 18.4 %fusion.76 = f32[128,512]{1,0:T(8,128)S(1)} fusion(f32[512,128]{0,1:T(8,128)S(1)} %fusion.75, f32[128,2048]{1,0:T(8,128)S(1)} %copy-done.16, s32[512]{0:T(512)S(1)} %iota_add_fusion.3, s32[2048]{0:T(1024)S(1)} %get-tuple-element.340), kind=kOutput, calls=%fused_computation.19.clone.1 | convolution fusion | flops 1625358336 | bytes 1583104 | tf_op jit(solution)/shard_map/while/body/eval_jaxpr/dot_general | solution.py:63
  888.7 19.2 %convolution_subtract_fusion.2 = f32[128,2048]{1,0:T(8,128)S(1)} fusion(f32[128,512]{1,0:T(8,128)S(1)} %reshape.326, s32[512]{0:T(512)S(1)} %iota_add_fusion.3, s32[2048]{0:T(1024)S(1)} %get-tuple-element.340, f32[128,2048]{1,0:T(8,128)S(1)} %copy-done.13, pred[]{:T(512)S(6)} %compare.4), kind=kOutput, calls=%fused_computation.12.clone.1 | convolution fusion | flops 1625817088 | bytes 2369537 | tf_op jit(solution)/shard_map/while/body/eval_jaxpr/dot_general | solution.py:83
  908.0 19.5 %convolution_add_fusion.2 = f32[128,2048]{1,0:T(8,128)S(1)} fusion(f32[128,512]{1,0:T(8,128)S(1)} %reshape.326, s32[512]{0:T(512)S(1)} %iota_add_fusion.3, s32[2048]{0:T(1024)S(1)} %get-tuple-element.340, f32[128,2048]{1,0:T(8,128)S(1)} %copy-done.11, pred[]{:T(512)S(6)} %compare.4), kind=kOutput, calls=%fused_computation.13.clone.1 | convolution fusion | flops 1625817088 | bytes 2369537 | tf_op jit(solution)/shard_map/while/body/eval_jaxpr/dot_general | solution.py:76
  930.9 19.4 %fusion.75 = f32[512,128]{0,1:T(8,128)S(1)} fusion(f32[128,2048]{1,0:T(8,128)} %get-tuple-element.341, s32[512]{0:T(512)S(1)} %iota_add_fusion.3, s32[2048]{0:T(1024)S(1)} %get-tuple-element.340), kind=kOutput, calls=%fused_computation.16.clone.1 | convolution fusion | flops 1625292800 | bytes 1320960 | tf_op jit(solution)/shard_map/while/body/eval_jaxpr/dot_general | solution.py:57
  950.3 18.2 %fusion.76 = f32[128,512]{1,0:T(8,128)S(1)} fusion(f32[512,128]{0,1:T(8,128)S(1)} %fusion.75, f32[128,2048]{1,0:T(8,128)S(1)} %copy-done.16, s32[512]{0:T(512)S(1)} %iota_add_fusion.3, s32[2048]{0:T(1024)S(1)} %get-tuple-element.340), kind=kOutput, calls=%fused_computation.19.clone.1 | convolution fusion | flops 1625358336 | bytes 1583104 | tf_op jit(solution)/shard_map/while/body/eval_jaxpr/dot_general | solution.py:63
  969.5 19.4 %convolution_subtract_fusion.2 = f32[128,2048]{1,0:T(8,128)S(1)} fusion(f32[128,512]{1,0:T(8,128)S(1)} %reshape.326, s32[512]{0:T(512)S(1)} %iota_add_fusion.3, s32[2048]{0:T(1024)S(1)} %get-tuple-element.340, f32[128,2048]{1,0:T(8,128)S(1)} %copy-done.13, pred[]{:T(512)S(6)} %compare.4), kind=kOutput, calls=%fused_computation.12.clone.1 | convolution fusion | flops 1625817088 | bytes 2369537 | tf_op jit(solution)/shard_map/while/body/eval_jaxpr/dot_general | solution.py:83
  989.0 19.3 %convolution_add_fusion.2 = f32[128,2048]{1,0:T(8,128)S(1)} fusion(f32[128,512]{1,0:T(8,128)S(1)} %reshape.326, s32[512]{0:T(512)S(1)} %iota_add_fusion.3, s32[2048]{0:T(1024)S(1)} %get-tuple-element.340, f32[128,2048]{1,0:T(8,128)S(1)} %copy-done.11, pred[]{:T(512)S(6)} %compare.4), kind=kOutput, calls=%fused_computation.13.clone.1 | convolution fusion | flops 1625817088 | bytes 2369537 | tf_op jit(solution)/shard_map/while/body/eval_jaxpr/dot_general | solution.py:76
  1023.7 14.8 %copy.102 = bf16[16,4,2,2048,2]{0,4,3,2,1:T(2,128)(2,1)} copy(bf16[16,4,2,2048,2]{3,2,1,0,4:T(2,128)(2,1)S(1)} %pad_maximum_fusion.1) | data formatting | bytes 2097152 | tf_op jit(solution)/shard_map/stack | solution.py:104
  1038.4 16.4 %copy.117 = bf16[16,4,2,4096,1]{0,2,1,4,3:T(2,128)(2,1)} copy(bf16[16,4,2,4096,1]{0,3,2,1,4:T(8,128)(2,1)} %bitcast.76) | data formatting | bytes 2097152 | tf_op jit(solution)/shard_map/convert_element_type | solution.py:108
  1065.2 22.2 %all_to_all.30 = bf16[32,2,8192]{2,1,0:T(2,128)(2,1)S(1)} all-to-all(bf16[32,2,8192]{2,1,0:T(2,128)(2,1)S(1)} %reshape.321), channel_id=1, replica_groups=mesh['row'=4,'ma'=32] {'ma'}, dimensions={0} | all-to-all | bytes 2097152 | tf_op jit(solution)/shard_map/all_to_all | solution.py:161
  1112.9 17.0 %copy.106 = bf16[64,16,2,2,128]{4,1,3,2,0:T(8,128)(2,1)} copy(bf16[64,16,2,2,128]{1,3,0,2,4:T(2,128)(2,1)} %bitcast.74) | data formatting | bytes 2097152 | tf_op jit(solution)/shard_map/transpose | solution.py:163
  1130.9 46.3 %all-gather.2.cloned.1.call-done = bf16[64,64,4,128]{3,1,2,0:T(8,128)(2,1)} async-done(((bf16[64,16,4,128]{3,1,2,0:T(8,128)(2,1)}), bf16[64,64,4,128]{3,1,2,0:T(8,128)(2,1)}) %all-gather.2.cloned.1.call-update) | async-done | bytes 4194320 | tf_op jit(solution)/shard_map/all_gather | solution.py:167
  1189.8 20.5 %fusion.47 = f32[64,256,512]{2,1,0:T(8,128)} fusion(bf16[64,256,128]{2,1,0:T(8,128)(2,1)} %bitcast.78, bf16[64,128,512]{2,1,0:T(8,128)(2,1)} %param.12), kind=kOutput, calls=%fused_computation.77 | convolution fusion | flops 2147483648 | bytes 46137344 | tf_op jit(solution)/shard_map/dot_general | solution.py:117
  1210.3 39.0 %reshape.291 = f32[64,64,2,2,512]{4,3,2,1,0:T(2,128)} reshape(f32[64,256,512]{2,1,0:T(8,128)} %fusion.47) | data formatting | bytes 67108864 | tf_op jit(solution)/shard_map/reshape | solution.py:120
  1249.3 20.5 %fusion.41 = f32[64,2,512]{2,1,0:T(2,128)S(1)} fusion(f32[64,64,2,2,512]{4,3,2,1,0:T(2,128)} %reshape.291, f32[64,512]{1,0:T(8,128)S(1)} %get-tuple-element.263, f32[64,512]{1,0:T(8,128)S(1)} %get-tuple-element.264), kind=kLoop, calls=%fused_computation.50 | loop fusion | flops 16711680 | bytes 34078720 | tf_op jit(solution)/shard_map/reduce_sum | solution.py:124
  (222 shorter events, 129.6 us)
Async XLA Ops:
  6.5 53.7 %copy-start = (f32[64,512]{1,0:T(8,128)S(1)}, f32[64,512]{1,0:T(8,128)}, u32[]{:S(2)}) copy-start(f32[64,512]{1,0:T(8,128)} %param.13) | copy-start | bytes 393220
  6.5 244.5 %all-reduce.2.cloned.1.call-start = ((), (), s32[]{:S(2)}) async-start(), calls=%async_computation.2 | async-start | bytes 16777216 | tf_op jit(solution)/shard_map/psum | solution.py:151
  20.4 39.8 %copy-start.21 = (s32[64]{0:T(128)S(1)}, s32[64]{0:T(128)}, u32[]{:S(2)}) copy-start(s32[64]{0:T(128)} %param.16) | copy-start | bytes 772
  20.4 40.5 %copy-start.3 = (f32[64,512]{1,0:T(8,128)S(1)}, f32[64,512]{1,0:T(8,128)}, u32[]{:S(2)}) copy-start(f32[64,512]{1,0:T(8,128)} %param.14) | copy-start | bytes 393220
  61.6 20.9 %copy-start.9 = (f32[64,512]{1,0:T(8,128)}, f32[64,512]{1,0:T(8,128)S(1)}, u32[]{:S(2)}) copy-start(f32[64,512]{1,0:T(8,128)S(1)} %gather_fusion.1) | copy-start | bytes 393220
  252.8 12.0 copy-start.17
  252.8 12.0 copy-start.19
  255.3 37.6 %all-to-all-start = ((f32[16,128,2,1,128]{4,3,2,0,1:T(1,128)}), f32[16,128,2,1,128]{4,3,2,0,1:T(1,128)}, u32[]{:S(2)}, u32[]{:S(2)}) async-start(f32[16,128,2,1,128]{4,3,2,0,1:T(1,128)} %copy.97), calls=%async_computation | async-start | bytes 4194304 | tf_op jit(solution)/shard_map/all_to_all | solution.py:156
  264.2 913.1 %all-gather.2.cloned.1.call-start = ((), (), s32[]{:S(2)}) async-start(), calls=%async_computation.3 | async-start | bytes 5242880 | tf_op jit(solution)/shard_map/all_gather | solution.py:167
  342.2 19.3 %copy-start.4 = (f32[128,2048]{1,0:T(8,128)S(1)}, f32[128,2048]{1,0:T(8,128)}, u32[]{:S(2)}) copy-start(f32[128,2048]{1,0:T(8,128)} %mul.390) | copy-start | bytes 3145732
  365.0 19.2 %copy-start.16 = (f32[128,2048]{1,0:T(8,128)S(1)}, f32[128,2048]{1,0:T(8,128)}, u32[]{:S(2)}) copy-start(f32[128,2048]{1,0:T(8,128)} %get-tuple-element.342) | copy-start | bytes 3145732 | tf_op jit(solution)/shard_map/while
  384.2 19.3 %copy-start.13 = (f32[128,2048]{1,0:T(8,128)S(1)}, f32[128,2048]{1,0:T(8,128)}, u32[]{:S(2)}) copy-start(f32[128,2048]{1,0:T(8,128)} %get-tuple-element.328) | copy-start | bytes 3145732 | tf_op jit(solution)/shard_map/while
  403.6 19.3 %copy-start.11 = (f32[128,2048]{1,0:T(8,128)S(1)}, f32[128,2048]{1,0:T(8,128)}, u32[]{:S(2)}) copy-start(f32[128,2048]{1,0:T(8,128)} %get-tuple-element.327) | copy-start | bytes 3145732 | tf_op jit(solution)/shard_map/while
  422.8 19.5 %copy-start.14 = (f32[128,2048]{1,0:T(8,128)}, f32[128,2048]{1,0:T(8,128)S(1)}, u32[]{:S(2)}) copy-start(f32[128,2048]{1,0:T(8,128)S(1)} %convolution_subtract_fusion.2) | copy-start | bytes 3145732 | tf_op jit(solution)/shard_map/while
  445.8 19.4 %copy-start.16 = (f32[128,2048]{1,0:T(8,128)S(1)}, f32[128,2048]{1,0:T(8,128)}, u32[]{:S(2)}) copy-start(f32[128,2048]{1,0:T(8,128)} %get-tuple-element.342) | copy-start | bytes 3145732 | tf_op jit(solution)/shard_map/while
  465.2 19.1 %copy-start.13 = (f32[128,2048]{1,0:T(8,128)S(1)}, f32[128,2048]{1,0:T(8,128)}, u32[]{:S(2)}) copy-start(f32[128,2048]{1,0:T(8,128)} %get-tuple-element.328) | copy-start | bytes 3145732 | tf_op jit(solution)/shard_map/while
  484.4 19.5 %copy-start.11 = (f32[128,2048]{1,0:T(8,128)S(1)}, f32[128,2048]{1,0:T(8,128)}, u32[]{:S(2)}) copy-start(f32[128,2048]{1,0:T(8,128)} %get-tuple-element.327) | copy-start | bytes 3145732 | tf_op jit(solution)/shard_map/while
  503.8 19.3 %copy-start.14 = (f32[128,2048]{1,0:T(8,128)}, f32[128,2048]{1,0:T(8,128)S(1)}, u32[]{:S(2)}) copy-start(f32[128,2048]{1,0:T(8,128)S(1)} %convolution_subtract_fusion.2) | copy-start | bytes 3145732 | tf_op jit(solution)/shard_map/while
  526.8 19.2 %copy-start.16 = (f32[128,2048]{1,0:T(8,128)S(1)}, f32[128,2048]{1,0:T(8,128)}, u32[]{:S(2)}) copy-start(f32[128,2048]{1,0:T(8,128)} %get-tuple-element.342) | copy-start | bytes 3145732 | tf_op jit(solution)/shard_map/while
  546.0 19.4 %copy-start.13 = (f32[128,2048]{1,0:T(8,128)S(1)}, f32[128,2048]{1,0:T(8,128)}, u32[]{:S(2)}) copy-start(f32[128,2048]{1,0:T(8,128)} %get-tuple-element.328) | copy-start | bytes 3145732 | tf_op jit(solution)/shard_map/while
  565.4 19.2 %copy-start.11 = (f32[128,2048]{1,0:T(8,128)S(1)}, f32[128,2048]{1,0:T(8,128)}, u32[]{:S(2)}) copy-start(f32[128,2048]{1,0:T(8,128)} %get-tuple-element.327) | copy-start | bytes 3145732 | tf_op jit(solution)/shard_map/while
  584.6 19.6 %copy-start.14 = (f32[128,2048]{1,0:T(8,128)}, f32[128,2048]{1,0:T(8,128)S(1)}, u32[]{:S(2)}) copy-start(f32[128,2048]{1,0:T(8,128)S(1)} %convolution_subtract_fusion.2) | copy-start | bytes 3145732 | tf_op jit(solution)/shard_map/while
  607.5 19.2 %copy-start.16 = (f32[128,2048]{1,0:T(8,128)S(1)}, f32[128,2048]{1,0:T(8,128)}, u32[]{:S(2)}) copy-start(f32[128,2048]{1,0:T(8,128)} %get-tuple-element.342) | copy-start | bytes 3145732 | tf_op jit(solution)/shard_map/while
  626.8 19.3 %copy-start.13 = (f32[128,2048]{1,0:T(8,128)S(1)}, f32[128,2048]{1,0:T(8,128)}, u32[]{:S(2)}) copy-start(f32[128,2048]{1,0:T(8,128)} %get-tuple-element.328) | copy-start | bytes 3145732 | tf_op jit(solution)/shard_map/while
  646.1 19.3 %copy-start.11 = (f32[128,2048]{1,0:T(8,128)S(1)}, f32[128,2048]{1,0:T(8,128)}, u32[]{:S(2)}) copy-start(f32[128,2048]{1,0:T(8,128)} %get-tuple-element.327) | copy-start | bytes 3145732 | tf_op jit(solution)/shard_map/while
  665.4 19.5 %copy-start.14 = (f32[128,2048]{1,0:T(8,128)}, f32[128,2048]{1,0:T(8,128)S(1)}, u32[]{:S(2)}) copy-start(f32[128,2048]{1,0:T(8,128)S(1)} %convolution_subtract_fusion.2) | copy-start | bytes 3145732 | tf_op jit(solution)/shard_map/while
  688.3 19.4 %copy-start.16 = (f32[128,2048]{1,0:T(8,128)S(1)}, f32[128,2048]{1,0:T(8,128)}, u32[]{:S(2)}) copy-start(f32[128,2048]{1,0:T(8,128)} %get-tuple-element.342) | copy-start | bytes 3145732 | tf_op jit(solution)/shard_map/while
  707.8 19.1 %copy-start.13 = (f32[128,2048]{1,0:T(8,128)S(1)}, f32[128,2048]{1,0:T(8,128)}, u32[]{:S(2)}) copy-start(f32[128,2048]{1,0:T(8,128)} %get-tuple-element.328) | copy-start | bytes 3145732 | tf_op jit(solution)/shard_map/while
  726.9 19.5 %copy-start.11 = (f32[128,2048]{1,0:T(8,128)S(1)}, f32[128,2048]{1,0:T(8,128)}, u32[]{:S(2)}) copy-start(f32[128,2048]{1,0:T(8,128)} %get-tuple-element.327) | copy-start | bytes 3145732 | tf_op jit(solution)/shard_map/while
  746.4 19.3 %copy-start.14 = (f32[128,2048]{1,0:T(8,128)}, f32[128,2048]{1,0:T(8,128)S(1)}, u32[]{:S(2)}) copy-start(f32[128,2048]{1,0:T(8,128)S(1)} %convolution_subtract_fusion.2) | copy-start | bytes 3145732 | tf_op jit(solution)/shard_map/while
  769.3 19.2 %copy-start.16 = (f32[128,2048]{1,0:T(8,128)S(1)}, f32[128,2048]{1,0:T(8,128)}, u32[]{:S(2)}) copy-start(f32[128,2048]{1,0:T(8,128)} %get-tuple-element.342) | copy-start | bytes 3145732 | tf_op jit(solution)/shard_map/while
  788.5 19.4 %copy-start.13 = (f32[128,2048]{1,0:T(8,128)S(1)}, f32[128,2048]{1,0:T(8,128)}, u32[]{:S(2)}) copy-start(f32[128,2048]{1,0:T(8,128)} %get-tuple-element.328) | copy-start | bytes 3145732 | tf_op jit(solution)/shard_map/while
  807.9 19.2 %copy-start.11 = (f32[128,2048]{1,0:T(8,128)S(1)}, f32[128,2048]{1,0:T(8,128)}, u32[]{:S(2)}) copy-start(f32[128,2048]{1,0:T(8,128)} %get-tuple-element.327) | copy-start | bytes 3145732 | tf_op jit(solution)/shard_map/while
  827.1 19.6 %copy-start.14 = (f32[128,2048]{1,0:T(8,128)}, f32[128,2048]{1,0:T(8,128)S(1)}, u32[]{:S(2)}) copy-start(f32[128,2048]{1,0:T(8,128)S(1)} %convolution_subtract_fusion.2) | copy-start | bytes 3145732 | tf_op jit(solution)/shard_map/while
  850.1 19.2 %copy-start.16 = (f32[128,2048]{1,0:T(8,128)S(1)}, f32[128,2048]{1,0:T(8,128)}, u32[]{:S(2)}) copy-start(f32[128,2048]{1,0:T(8,128)} %get-tuple-element.342) | copy-start | bytes 3145732 | tf_op jit(solution)/shard_map/while
  869.3 19.3 %copy-start.13 = (f32[128,2048]{1,0:T(8,128)S(1)}, f32[128,2048]{1,0:T(8,128)}, u32[]{:S(2)}) copy-start(f32[128,2048]{1,0:T(8,128)} %get-tuple-element.328) | copy-start | bytes 3145732 | tf_op jit(solution)/shard_map/while
  888.7 19.3 %copy-start.11 = (f32[128,2048]{1,0:T(8,128)S(1)}, f32[128,2048]{1,0:T(8,128)}, u32[]{:S(2)}) copy-start(f32[128,2048]{1,0:T(8,128)} %get-tuple-element.327) | copy-start | bytes 3145732 | tf_op jit(solution)/shard_map/while
  907.9 19.5 %copy-start.14 = (f32[128,2048]{1,0:T(8,128)}, f32[128,2048]{1,0:T(8,128)S(1)}, u32[]{:S(2)}) copy-start(f32[128,2048]{1,0:T(8,128)S(1)} %convolution_subtract_fusion.2) | copy-start | bytes 3145732 | tf_op jit(solution)/shard_map/while
  930.9 19.4 %copy-start.16 = (f32[128,2048]{1,0:T(8,128)S(1)}, f32[128,2048]{1,0:T(8,128)}, u32[]{:S(2)}) copy-start(f32[128,2048]{1,0:T(8,128)} %get-tuple-element.342) | copy-start | bytes 3145732 | tf_op jit(solution)/shard_map/while
  950.3 19.1 %copy-start.13 = (f32[128,2048]{1,0:T(8,128)S(1)}, f32[128,2048]{1,0:T(8,128)}, u32[]{:S(2)}) copy-start(f32[128,2048]{1,0:T(8,128)} %get-tuple-element.328) | copy-start | bytes 3145732 | tf_op jit(solution)/shard_map/while
  969.5 19.5 %copy-start.11 = (f32[128,2048]{1,0:T(8,128)S(1)}, f32[128,2048]{1,0:T(8,128)}, u32[]{:S(2)}) copy-start(f32[128,2048]{1,0:T(8,128)} %get-tuple-element.327) | copy-start | bytes 3145732 | tf_op jit(solution)/shard_map/while
  988.9 19.3 %copy-start.14 = (f32[128,2048]{1,0:T(8,128)}, f32[128,2048]{1,0:T(8,128)S(1)}, u32[]{:S(2)}) copy-start(f32[128,2048]{1,0:T(8,128)S(1)} %convolution_subtract_fusion.2) | copy-start | bytes 3145732 | tf_op jit(solution)/shard_map/while
  1018.0 2.7 copy-start.20
  1112.9 17.0 %copy-start.2 = (f32[64]{0:T(128)S(1)}, f32[64]{0:T(128)}, u32[]{:S(2)}) copy-start(f32[64]{0:T(128)} %param.15) | copy-start | bytes 772
  1112.9 17.9 %copy-start.8 = (f32[64,512]{1,0:T(8,128)S(1)}, f32[64,512]{1,0:T(8,128)}, u32[]{:S(2)}) copy-start(f32[64,512]{1,0:T(8,128)} %copy-done.7) | copy-start | bytes 393220
  1112.9 17.9 %copy-start.10 = (f32[64,512]{1,0:T(8,128)S(1)}, f32[64,512]{1,0:T(8,128)}, u32[]{:S(2)}) copy-start(f32[64,512]{1,0:T(8,128)} %copy-done.9) | copy-start | bytes 393220
  1249.3 20.5 %copy-start.6 = (f32[64,512]{1,0:T(8,128)S(1)}, f32[64,512]{1,0:T(8,128)}, u32[]{:S(2)}) copy-start(f32[64,512]{1,0:T(8,128)} %copy-done.5) | copy-start | bytes 393220
  1249.3 21.4 %copy-start.1 = (f32[64,512]{1,0:T(8,128)S(1)}, f32[64,512]{1,0:T(8,128)}, u32[]{:S(2)}) copy-start(f32[64,512]{1,0:T(8,128)} %param.13) | copy-start | bytes 393220
  (12 other events, 12.9 us)
Sparse Core Ops, SparseCore 0:
  90.5 160.4 all-reduce.1
  1130.0 47.1 all-gather.1
where the time goes:
time: 1290 us; the launch traced here: 1280 us
  matrix products  652 us (51%)
  local copies, waits for them, and re-layouts  288 us (22%)
  waiting for transfers between devices  231 us (18%)
  other arithmetic  34.2 us (3%)
  loops' own time  27.4 us (2%)
  blocking collectives  22.2 us (2%)
  between operations  14.1 us (1%)
    psum x1, waiting for transfers between devices, body(): lax.psum(synth_rows(radius_count, coeff_rows, alpha_table, beta_table, ra...  161 us
    dot_general x8, matrix products, block_step(): lax.dot_general(products, cos_table, contract, precision=lax.Precision.HI...  155 us
    dot_general x8, matrix products, block_step(): lax.dot_general(products, sin_table, contract, precision=lax.Precision.HI...  154 us
    dot_general x8, matrix products, block_step(): jnp.dot(rotated_re, cos_table, precision=lax.Precision.HIGHEST, preferred...  154 us
    dot_general x8, matrix products, block_step(): jnp.dot(rotated_im, sin_table, precision=lax.Precision.HIGHEST, preferred...  147 us
    mul x4, local copies, waits for them, and re-layouts, synth_rows(): filters[None, :, :, None, :] * coeff_rows[:, None, None, :, :]  51.5 us
    all_gather x1, waiting for transfers between devices, body(): lax.all_gather(returned, 'row', axis=1, tiled=True)  46.3 us
    reshape x1, local copies, waits for them, and re-layouts, adjoint_rows(): adjoint_terms.reshape(local_orders, row_count, 2, 2, local_degrees)  39 us
  transfers between devices with their start and end apart: 3, of which 3 were waited for; matrix products, arithmetic and copies ran while one was open for 0% of the time, Pallas kernels for 0%

commit v1 on v0

v1 whole, which is shorter than its diff:
```python
import functools

import jax
import jax.numpy as jnp
import ml_dtypes
import numpy as np
from jax import lax
from jax.experimental import pallas as pl
from jax.experimental.pallas import tpu as pltpu
from jax.sharding import PartitionSpec as P

NPIX = 4096
SIDE = 64
BLOCKS = 32
BF16 = jnp.bfloat16
F32 = jnp.float32


def split_np(table):
    high = table.astype(ml_dtypes.bfloat16)
    low = (table - high.astype(np.float64)).astype(ml_dtypes.bfloat16)
    return high, low


def dft_tables():
    p1 = np.arange(SIDE)
    first, first_t, second, second_t = [], [], [], []
    for offset in (0, 1):
        b = np.arange(BLOCKS)
        angle = (np.outer(2 * p1 + offset, b) % 128) * (2.0 * np.pi / 128)
        cos, sin = 2.0 * np.cos(angle), 2.0 * np.sin(angle)
        stage = np.block([[cos, -sin], [sin, cos]])
        high, low = split_np(stage)
        first.append(np.concatenate([high, high, low], axis=1))
        first_t.append(np.concatenate([high.T, high.T, low.T], axis=1))
        j = np.arange(SIDE)
        p2 = np.arange(SIDE)
        steps = (2 * p1[:, None] + offset + 128 * p2[None, :])[:, :, None] * j
        angle = (steps % 8192) * (2.0 * np.pi / 8192)
        stage = np.stack([np.cos(angle), -np.sin(angle)], axis=-1).reshape(SIDE, SIDE, 2 * SIDE)
        high, low = split_np(stage)
        second.append(np.concatenate([high, high, low], axis=2))
        high, low = (np.swapaxes(part, 1, 2) for part in (high, low))
        second_t.append(np.concatenate([high, high, low], axis=2))
    return [np.stack(tables) for tables in (first, first_t, second, second_t)]


def split(values):
    high = values.astype(BF16)
    low = (values - high.astype(F32)).astype(BF16)
    return high, low


def place(order):
    return 2 * lax.shift_right_logical(order, 6) + lax.bitwise_and(order, 1)


def synth_kernel(meta, nodes, coeffs_ref, alpha_ref, beta_ref, leg_ref, out_ref, filters, acc_re, acc_im):
    slots, cycles, degrees = leg_ref.shape
    radii = nodes.shape[0]

    def fill(r, _):
        filters[pl.ds(r, 1), :] = alpha_ref[pl.ds(nodes[r], 1), :]
        filters[pl.ds(radii + r, 1), :] = beta_ref[pl.ds(nodes[r], 1), :]
        return 0

    lax.fori_loop(0, radii, fill, 0, unroll=8)
    degree = meta[0] + lax.broadcasted_iota(jnp.int32, (1, degrees), 1)

    def step(s, _):
        order = meta[1 + s]
        live = degree >= order
        parts = []
        for c in range(2):
            row = jnp.where(live, coeffs_ref[c, pl.ds(s, 1), :], 0.0)
            parts.append((filters[...] * row).astype(BF16))
        filtered = jnp.concatenate(parts, axis=0)
        harmonic = lax.dot_general(
            leg_ref[s], filtered, (((1,), (1,)), ((), ())), preferred_element_type=F32
        )
        at = pl.ds(place(order), cycles, stride=slots)
        acc_re[at, :] = harmonic[:, : 2 * radii]
        acc_im[at, :] = harmonic[:, 2 * radii :]
        return 0

    lax.fori_loop(0, slots, step, 0, unroll=2)

    def finish(g, _):
        rows = pl.ds(pl.multiple_of(g * slots, slots), slots)
        out_ref[g, :, : 2 * radii] = acc_re[rows, :].astype(BF16)
        out_ref[g, :, 2 * radii :] = acc_im[rows, :].astype(BF16)
        return 0

    lax.fori_loop(0, cycles, finish, 0, unroll=4)


def cycle_kernel(
    offset, parts_ref, place_ref, weight_ref, first_ref, first_t_ref, second_ref, second_t_ref,
    out_ref, sum_re, sum_im, spectra, middle, products, middle_t, back_re, back_im,
):
    owners, slots, width = out_ref.shape
    half = width // 2
    rows_total = parts_ref.shape[0] // owners

    def gather(a, _):
        total = parts_ref[a * rows_total].astype(F32)
        for row in range(1, rows_total):
            total = total + parts_ref[a * rows_total + row].astype(F32)
        rows = pl.ds(pl.multiple_of(a * slots, slots), slots)
        sum_re[rows, :] = total[:, :half]
        sum_im[rows, :] = total[:, half:]
        return 0

    lax.fori_loop(0, owners, gather, 0, unroll=2)
    row_j = lax.broadcasted_iota(jnp.int32, (SIDE, 2 * SIDE), 0)

    def sort(b, _):
        pick = row_j == place_ref[pl.ds(b, 1), :]
        one = jnp.where((row_j == 0) & (b == 0), 0.5, 1.0)
        table = jnp.where(pick, one, 0.0).astype(BF16)
        terms = []
        for source in (sum_re, sum_im):
            values = jnp.concatenate(
                [source[pl.ds(2 * b + h, owners, stride=slots), :] for h in range(2)], axis=0
            )
            terms.append(jnp.concatenate(split(values), axis=0))
        placed = jnp.dot(table, jnp.concatenate(terms, axis=1), preferred_element_type=F32)
        spectra[pl.ds(b, SIDE, stride=SIDE), :] = placed[:, :half]
        spectra[pl.ds(BLOCKS + b, SIDE, stride=SIDE), :] = placed[:, half:]
        return 0

    lax.fori_loop(0, BLOCKS, sort, 0, unroll=2)

    def synth_first(k, _):
        pair = []
        for e in range(2):
            high, low = split(spectra[pl.ds(pl.multiple_of((2 * k + e) * SIDE, SIDE), SIDE), :])
            pair.append(jnp.concatenate([high, low, high], axis=0))
        out = jnp.dot(first_ref[0], jnp.concatenate(pair, axis=1), preferred_element_type=F32)
        for e in range(2):
            rows = pl.ds(pl.multiple_of((2 * k + e) * 2 * SIDE, 2 * SIDE), 2 * SIDE)
            middle[rows, :] = out[:, e * half : (e + 1) * half]
        return 0

    lax.fori_loop(0, SIDE // 2, synth_first, 0, unroll=2)
    lower = lax.broadcasted_iota(jnp.int32, (SIDE, half), 1) < half // 2

    def synth_second(k, total):
        high, low = split(middle[pl.ds(k, 2 * SIDE, stride=SIDE), :])
        values = jnp.concatenate([high, low, high], axis=0)
        fields = jnp.dot(second_ref[0, k], values, preferred_element_type=F32)
        swapped = pltpu.roll(fields, half // 2, 1)
        product = swapped * jnp.where(lower, swapped, fields)
        product = jnp.where(lower, product, swapped * fields)
        products[k] = product
        return total + product

    total = lax.fori_loop(0, SIDE, synth_second, jnp.zeros((SIDE, half), F32), unroll=2)
    mean = jnp.sum(total, axis=0, keepdims=True) * (1.0 / NPIX)

    def analyse_second(k, _):
        high, low = split(products[k] - mean)
        values = jnp.concatenate([high, low, high], axis=0)
        out = jnp.dot(second_t_ref[0, k], values, preferred_element_type=F32)
        middle_t[pl.ds(k, 2 * SIDE, stride=SIDE), :] = out
        return 0

    lax.fori_loop(0, SIDE, analyse_second, 0, unroll=2)
    scale = weight_ref[0] * 0.5

    def analyse_first(k, _):
        pair = []
        for e in range(2):
            rows = pl.ds(pl.multiple_of((2 * k + e) * 2 * SIDE, 2 * SIDE), 2 * SIDE)
            high, low = split(middle_t[rows, :])
            pair.append(jnp.concatenate([high, low, high], axis=0))
        out = jnp.dot(first_t_ref[0], jnp.concatenate(pair, axis=1), preferred_element_type=F32)
        for e in range(2):
            rows = pl.ds(pl.multiple_of((2 * k + e) * SIDE, SIDE), SIDE)
            spectra[rows, :] = out[:, e * half : (e + 1) * half] * scale
        return 0

    lax.fori_loop(0, SIDE // 2, analyse_first, 0, unroll=2)

    def unsort(b, _):
        pick = row_j == place_ref[pl.ds(b, 1), :]
        table = jnp.where(pick, 1.0, 0.0)[:, :SIDE].astype(BF16)
        values = jnp.concatenate(
            [spectra[pl.ds(c * BLOCKS + b, SIDE, stride=SIDE), :].astype(BF16) for c in range(2)],
            axis=1,
        )
        out = lax.dot_general(
            table, values, (((0,), (0,)), ((), ())), preferred_element_type=F32
        )
        for h in range(2):
            at = pl.ds(2 * b + h, owners, stride=slots)
            back_re[at, :] = out[h * owners : (h + 1) * owners, :half]
            back_im[at, :] = out[h * owners : (h + 1) * owners, half:]
        return 0

    lax.fori_loop(0, BLOCKS, unsort, 0, unroll=2)

    def finish(a, _):
        rows = pl.ds(pl.multiple_of(a * slots, slots), slots)
        out_ref[a, :, :half] = back_re[rows, :].astype(BF16)
        out_ref[a, :, half:] = back_im[rows, :].astype(BF16)
        return 0

    lax.fori_loop(0, owners, finish, 0, unroll=4)


def adjoint_kernel(
    meta, nodes, radial, alpha_ref, beta_ref, leg_ref, parts_ref, out_ref, filters, weights, in_re, in_im
):
    slots, cycles, degrees = leg_ref.shape
    radii = nodes.shape[0]

    def fill(r, _):
        node = nodes[r]
        filters[pl.ds(r, 1), :] = alpha_ref[pl.ds(node, 1), :] * radial[node]
        filters[pl.ds(radii + r, 1), :] = beta_ref[pl.ds(node, 1), :] * (2.0 * radial[node])
        return 0

    lax.fori_loop(0, radii, fill, 0, unroll=8)
    high, low = split(filters[...])
    weights[: 2 * radii, :] = high
    weights[2 * radii :, :] = low
    degree = meta[0] + lax.broadcasted_iota(jnp.int32, (1, degrees), 1)

    def widen(g, _):
        rows = pl.ds(pl.multiple_of(g * slots, slots), slots)
        in_re[rows, :] = parts_ref[g, :, : 2 * radii].astype(F32)
        in_im[rows, :] = parts_ref[g, :, 2 * radii :].astype(F32)
        return 0

    lax.fori_loop(0, cycles, widen, 0, unroll=4)

    def step(s, _):
        order = meta[1 + s]
        live = degree >= order
        at = pl.ds(place(order), cycles, stride=slots)
        legendre = leg_ref[s].astype(F32)
        for c, source in enumerate((in_re, in_im)):
            values = source[at, :].astype(BF16)
            values = jnp.concatenate([values, values], axis=1)
            summed = jnp.dot(values, weights[...], preferred_element_type=F32)
            row = jnp.sum(summed * legendre, axis=0, keepdims=True)
            out_ref[c, pl.ds(s, 1), :] = jnp.where(live, row, 0.0)
        return 0

    lax.fori_loop(0, slots, step, 0, unroll=2)


VMEM = pl.BlockSpec(memory_space=pltpu.VMEM)
SMEM = pl.BlockSpec(memory_space=pltpu.SMEM)


def params(mib):
    return pltpu.CompilerParams(vmem_limit_bytes=mib * 2**20)


def body(
    coeffs, legendre, alpha_table, beta_table, radial_weight, radius_index, orders, cycle_offset, cycle_weight
):
    row_id = lax.axis_index("row")
    ma_id = lax.axis_index("ma")
    ma_count = lax.axis_size("ma")
    row_count = lax.axis_size("row")
    slots, cycles, degrees = legendre.shape
    radii = radius_index.shape[0]
    width = 4 * radii
    my_orders = lax.dynamic_slice_in_dim(orders, ma_id * slots, slots)
    meta = jnp.concatenate([jnp.full((1,), row_id * degrees, jnp.int32), my_orders])
    own = (row_id,)
    offset = lax.dynamic_slice(cycle_offset, own, (1,))
    weight = lax.dynamic_slice(cycle_weight, own, (1,))

    of_owner = orders.reshape(ma_count, 1, slots)
    where = place(of_owner) == jnp.arange(slots, dtype=jnp.int32)[None, :, None]
    placed = jnp.sum(jnp.where(where, lax.bitwise_and(of_owner, SIDE - 1), 0), axis=2)
    placed = jnp.transpose(placed.reshape(ma_count, BLOCKS, 2), (1, 2, 0)).reshape(BLOCKS, SIDE)
    placed = jnp.concatenate([placed, placed], axis=1)

    harmonic = pl.pallas_call(
        synth_kernel,
        out_shape=jax.ShapeDtypeStruct((cycles, slots, width), BF16),
        in_specs=[SMEM, SMEM, VMEM, VMEM, VMEM, VMEM],
        out_specs=VMEM,
        scratch_shapes=[
            pltpu.VMEM((2 * radii, degrees), F32),
            pltpu.VMEM((cycles * slots, 2 * radii), F32),
            pltpu.VMEM((cycles * slots, 2 * radii), F32),
        ],
        compiler_params=params(48),
        name="synth",
    )(meta, radius_index, coeffs, alpha_table, beta_table, legendre)

    both = ("ma", "row")
    parts = lax.all_to_all(harmonic, both, split_axis=0, concat_axis=0, tiled=True)

    tables = [jnp.asarray(table) for table in dft_tables()]
    whole = lambda *shape: pl.BlockSpec(shape, lambda i, off: (0,) * len(shape))
    chosen = lambda table: pl.BlockSpec(
        (1,) + table.shape[1:], lambda i, off: (off[0],) + (0,) * (table.ndim - 1)
    )
    plane = lambda rows: pltpu.VMEM((rows, 2 * radii), F32)
    analysed = pl.pallas_call(
        cycle_kernel,
        out_shape=jax.ShapeDtypeStruct((ma_count, slots, width), BF16),
        grid_spec=pltpu.PrefetchScalarGridSpec(
            num_scalar_prefetch=1,
            grid=(1,),
            in_specs=[
                whole(*parts.shape),
                whole(*placed.shape),
                pl.BlockSpec(memory_space=pltpu.SMEM),
                *[chosen(table) for table in tables],
            ],
            out_specs=whole(ma_count, slots, width),
            scratch_shapes=[
                plane(ma_count * slots),
                plane(ma_count * slots),
                plane(SIDE * SIDE),
                plane(2 * SIDE * SIDE),
                pltpu.VMEM((SIDE, SIDE, 2 * radii), F32),
                plane(2 * SIDE * SIDE),
                plane(ma_count * slots),
                plane(ma_count * slots),
            ],
        ),
        compiler_params=params(60),
        name="cycle",
    )(offset, parts, placed, weight, *tables)

    spread = jnp.broadcast_to(analysed[:, None], (ma_count, row_count, slots, width))
    spread = spread.reshape(cycles, slots, width)
    returned = lax.all_to_all(spread, both, split_axis=0, concat_axis=0, tiled=True)

    return pl.pallas_call(
        adjoint_kernel,
        out_shape=jax.ShapeDtypeStruct((2, slots, degrees), F32),
        in_specs=[SMEM, SMEM, SMEM, VMEM, VMEM, VMEM, VMEM],
        out_specs=VMEM,
        scratch_shapes=[
            pltpu.VMEM((2 * radii, degrees), F32),
            pltpu.VMEM((4 * radii, degrees), BF16),
            pltpu.VMEM((cycles * slots, 2 * radii), F32),
            pltpu.VMEM((cycles * slots, 2 * radii), F32),
        ],
        compiler_params=params(48),
        name="adjoint",
    )(meta, radius_index, radial_weight, alpha_table, beta_table, legendre, returned)


def solution(mesh):
    in_specs = (
        P(None, "ma", "row"),
        P("ma", None, "row"),
        P(None, "row"),
        P(None, "row"),
        P(),
        P(),
        P(),
        P("ma"),
        P("ma"),
    )
    return jax.shard_map(
        body, mesh=mesh, in_specs=in_specs, out_specs=P(None, "ma", "row"), check_vma=False
    )
```

time: 1290 us -> 219 us (0.17)
  matrix products: 652 us -> 0 us
  local copies, waits for them, and re-layouts: 288 us -> 9.52 us
  waiting for transfers between devices: 231 us -> 50.8 us
  Pallas kernels: 0 us -> 83.1 us
  blocking collectives: 22.2 us -> 61.4 us
  other arithmetic: 34.2 us -> 1.39 us
  loops' own time: 27.4 us -> 0 us
  between operations: 14.1 us -> 0.1 us
    dot_general x34 -> x0, matrix products: 652 us -> none  [the longest x8 155 us: block_step(): lax.dot_general(products, cos_table, contract, precision=lax.Precision.HI...]
    psum x1 -> x0, waiting for transfers between devices: 161 us -> none  [body(): lax.psum(synth_rows(radius_count, coeff_rows, alpha_table, beta_table, ra...]
    pallas_call x0 -> x3, Pallas kernels: none -> 83.1 us  [the longest x1 41.3 us: body(): pl.pallas_call(cycle_kernel, out_shape=jax.ShapeDtypeStruct((ma_count, sl...]
    mul x9 -> x0, local copies, waits for them, and re-layouts: 55.7 us -> none  [the longest x4 51.5 us: synth_rows(): filters[None, :, :, None, :] * coeff_rows[:, None, None, :, :]]
    reshape x22 -> x1, local copies, waits for them, and re-layouts: 55 us -> 0.09 us  [body(): jnp.transpose(placed.reshape(ma_count, BLOCKS, 2), (1, 2, 0))]
    slice x3 -> x0, local copies, waits for them, and re-layouts: 54.4 us -> none  [the longest x2 36.9 us: cycle_work(): real_part = separated[..., 0]]
    all_gather x1 -> x0, waiting for transfers between devices: 46.3 us -> none  [body(): lax.all_gather(returned, 'row', axis=1, tiled=True)]
    all_to_all x1, blocking collectives: 22.2 us -> 61.4 us  [body(): lax.all_to_all(spread, both, split_axis=0, concat_axis=0, tiled=True)]
  transfers between devices with their start and end apart: 3 -> 1, of which waited for: 3 -> 1; matrix products, arithmetic and copies ran while one was open for 0% -> 1% of each run, Pallas kernels for 0% -> 0%
where the time goes in v1:
time: 219 us; the launch traced here: 217 us
  Pallas kernels  83.1 us (38%)
  blocking collectives  61.4 us (28%)
  waiting for transfers between devices  50.8 us (23%)
  starting transfers between devices  11.1 us (5%)
  local copies, waits for them, and re-layouts  9.52 us (4%)
    all_to_all x1, blocking collectives, body(): lax.all_to_all(spread, both, split_axis=0, concat_axis=0, tiled=True)  61.4 us
    all_to_all x1, waiting for transfers between devices, body(): lax.all_to_all(harmonic, both, split_axis=0, concat_axis=0, tiled=True)  50.8 us
    pallas_call x1, Pallas kernels, body(): pl.pallas_call(cycle_kernel, out_shape=jax.ShapeDtypeStruct((ma_count, sl...  41.3 us
    pallas_call x1, Pallas kernels, body(): pl.pallas_call(synth_kernel, out_shape=jax.ShapeDtypeStruct((cycles, slot...  21.6 us
    pallas_call x1, Pallas kernels, body(): pl.pallas_call(adjoint_kernel, out_shape=jax.ShapeDtypeStruct((2, slots,...  20.1 us
    all_to_all x1, starting transfers between devices, body(): lax.all_to_all(harmonic, both, split_axis=0, concat_axis=0, tiled=True)  11.1 us
    unnamed x24, local copies, waits for them, and re-layouts  5.4 us
  transfers between devices with their start and end apart: 1, of which 1 were waited for; matrix products, arithmetic and copies ran while one was open for 1% of the time, Pallas kernels for 0%

profile of v1, /device:TPU:15, one launch (start us, length us, event | category | flops | bytes accessed | tf_op | source)
XLA Modules:
  0.0 217.5 jit_solution(6374154506343628001)
XLA Ops:
  0.0 0.8 dynamic_slice.9
  0.8 0.1 pad_add_fusion.1.meta
  0.8 0.0 copy-start.1
  0.8 0.9 copy-done.1
  1.7 0.0 copy-start.3
  1.7 0.9 copy-done.3
  2.6 0.0 copy-start.5
  2.6 0.9 copy-done.5
  3.6 0.0 copy-start.6
  3.6 0.7 copy-done.6
  4.3 21.6 %synth.1 = bf16[128,64,256]{2,1,0:T(8,128)(2,1)S(1)} custom-call(s32[65]{0:T(128)S(1)} %pad_add_fusion.1.meta, s32[64]{0:T(128)S(1)} %copy-done.6, f32[2,64,512]{2,1,0:T(8,128)S(1)} %copy-done.5, f32[64,512]{1,0:T(8,128)S(1)} %copy-done.1, f32[64,512]{1,0:T(8,128)S(1)} %copy-done.3, bf16[64,128,512]{2,1,0:T(8,128)(2,1)} %leg_ref.3), custom_call_target="tpu_custom_call" | custom-call | tf_op jit(solution)/shard_map/synth/pallas_call | solution.py:284
  25.9 0.0 copy-start
  25.9 2.0 copy-done
  27.9 0.0 copy-start.10
  27.9 0.0 copy-start.11
  27.9 0.0 copy-start.9
  27.9 11.1 %all-to-all-start = ((bf16[128,64,256]{2,1,0:T(8,128)(2,1)}), bf16[128,64,256]{2,1,0:T(8,128)(2,1)}, u32[]{:S(2)}, u32[]{:S(2)}) async-start(bf16[128,64,256]{2,1,0:T(8,128)(2,1)} %copy-done), calls=%async_computation | async-start | bytes 8388608 | tf_op jit(solution)/shard_map/all_to_all | solution.py:299
  39.0 0.0 copy-done.10
  39.0 0.7 dynamic_slice.10.offset
  39.7 0.0 copy-done.11
  39.7 0.6 dynamic_slice.11.weight_ref
  40.3 0.0 copy-done.9
  40.4 0.1 add.21
  40.4 0.1 and.32
  40.5 0.6 select_reduce_fusion
  41.1 0.1 copy.15
  41.2 0.1 reshape.46
  41.3 0.7 pad_add_fusion.place_ref
  42.0 50.8 %all-to-all-done.parts_ref = bf16[128,64,256]{2,1,0:T(8,128)(2,1)} async-done(((bf16[128,64,256]{2,1,0:T(8,128)(2,1)}), bf16[128,64,256]{2,1,0:T(8,128)(2,1)}, u32[]{:S(2)}, u32[]{:S(2)}) %all-to-all-start) | async-done | bytes 4194336 | tf_op jit(solution)/shard_map/all_to_all | solution.py:299
  92.8 41.3 %cycle.1 = bf16[32,64,256]{2,1,0:T(8,128)(2,1)} custom-call(s32[1]{0:T(128)} %dynamic_slice.10.offset, bf16[128,64,256]{2,1,0:T(8,128)(2,1)} %all-to-all-done.parts_ref, s32[32,128]{1,0:T(8,128)} %pad_add_fusion.place_ref, f32[1]{0:T(128)} %dynamic_slice.11.weight_ref, bf16[2,128,192]{2,1,0:T(8,128)(2,1)} %constant.35.clone.first_ref, ...), custom_call_target="tpu_custom_call" | custom-call | tf_op jit(solution)/shard_map/cycle/pallas_call | solution.py:307
  134.1 1.7 broadcast_in_dim.25
  135.9 0.0 copy-start.2
  135.9 0.0 copy-start.4
  135.9 0.0 copy-start.7
  135.9 0.0 copy-start.8
  135.9 61.4 %all_to_all.10.parts_ref = bf16[128,64,256]{2,1,0:T(8,128)(2,1)S(1)} all-to-all(bf16[128,64,256]{2,1,0:T(8,128)(2,1)S(1)} %bitcast.5), channel_id=1, replica_groups=mesh['row'=4,'ma'=32] {'ma','row'}, dimensions={0} | all-to-all | bytes 8388608 | tf_op jit(solution)/shard_map/all_to_all | solution.py:337
  197.3 0.0 copy-done.2
  197.3 0.0 copy-done.4
  197.3 0.0 copy-done.7
  197.3 0.0 copy-done.8
  197.3 20.1 %adjoint.1 = f32[2,64,512]{2,1,0:T(8,128)} custom-call(s32[65]{0:T(128)S(1)} %pad_add_fusion.1.meta, s32[64]{0:T(128)S(1)} %copy-done.7, f32[64]{0:T(128)S(1)} %copy-done.8, f32[64,512]{1,0:T(8,128)S(1)} %copy-done.2, f32[64,512]{1,0:T(8,128)S(1)} %copy-done.4, bf16[64,128,512]{2,1,0:T(8,128)(2,1)} %leg_ref.3, bf16[128,64,256]{2,1,0:T(8,128)(2,1)S(1)} %all_to_all.10.parts_ref), custom_call_target="tpu_custom_call" | custom-call | tf_op jit(solution)/shard_map/adjoint/pallas_call | solution.py:339
  (1 shorter events, 0.0 us)
Async XLA Ops:
  0.8 0.9 copy-start.1
  1.7 0.9 copy-start.3
  2.6 0.9 copy-start.5
  3.6 0.7 copy-start.6
  25.9 2.0 copy-start
  27.9 11.2 %copy-start.10 = (s32[4]{0:T(128)S(1)}, s32[4]{0:T(128)}, u32[]{:S(2)}) copy-start(s32[4]{0:T(128)} %param.20) | copy-start | bytes 52
  27.9 11.8 %copy-start.11 = (f32[4]{0:T(128)S(1)}, f32[4]{0:T(128)}, u32[]{:S(2)}) copy-start(f32[4]{0:T(128)} %param.21) | copy-start | bytes 52
  27.9 12.5 %copy-start.9 = (s32[2048]{0:T(1024)S(1)}, s32[2048]{0:T(1024)}, u32[]{:S(2)}) copy-start(s32[2048]{0:T(1024)} %param.19) | copy-start | bytes 24580
  27.9 64.9 %all-to-all-start = ((bf16[128,64,256]{2,1,0:T(8,128)(2,1)}), bf16[128,64,256]{2,1,0:T(8,128)(2,1)}, u32[]{:S(2)}, u32[]{:S(2)}) async-start(bf16[128,64,256]{2,1,0:T(8,128)(2,1)} %copy-done), calls=%async_computation | async-start | bytes 8388608 | tf_op jit(solution)/shard_map/all_to_all | solution.py:299
  135.9 61.4 %copy-start.2 = (f32[64,512]{1,0:T(8,128)S(1)}, f32[64,512]{1,0:T(8,128)}, u32[]{:S(2)}) copy-start(f32[64,512]{1,0:T(8,128)} %alpha_ref.3) | copy-start | bytes 393220
  135.9 61.4 %copy-start.4 = (f32[64,512]{1,0:T(8,128)S(1)}, f32[64,512]{1,0:T(8,128)}, u32[]{:S(2)}) copy-start(f32[64,512]{1,0:T(8,128)} %beta_ref.3) | copy-start | bytes 393220
  135.9 61.4 %copy-start.7 = (s32[64]{0:T(128)S(1)}, s32[64]{0:T(128)}, u32[]{:S(2)}) copy-start(s32[64]{0:T(128)} %nodes.3) | copy-start | bytes 772
  135.9 61.4 %copy-start.8 = (f32[64]{0:T(128)S(1)}, f32[64]{0:T(128)}, u32[]{:S(2)}) copy-start(f32[64]{0:T(128)} %radial.1) | copy-start | bytes 772

commit v2 on v1

v2 whole, which is shorter than its diff:
```python
import functools

import jax
import jax.numpy as jnp
import ml_dtypes
import numpy as np
from jax import lax
from jax.experimental import pallas as pl
from jax.experimental.pallas import tpu as pltpu
from jax.sharding import PartitionSpec as P

NPIX = 4096
SIDE = 64
BLOCKS = 32
PITCH = 65
GROUP = 8
BF16 = jnp.bfloat16
F32 = jnp.float32


def split_np(table):
    high = table.astype(ml_dtypes.bfloat16)
    low = (table - high.astype(np.float64)).astype(ml_dtypes.bfloat16)
    return high, low


def dft_tables():
    p1 = np.arange(SIDE)
    first, first_t, second, second_t = [], [], [], []
    for offset in (0, 1):
        b = np.arange(BLOCKS)
        angle = (np.outer(2 * p1 + offset, b) % 128) * (2.0 * np.pi / 128)
        cos, sin = 2.0 * np.cos(angle), 2.0 * np.sin(angle)
        stage = np.block([[cos, -sin], [sin, cos]])
        high, low = split_np(stage)
        first.append(np.concatenate([high, high, low], axis=1))
        first_t.append(np.concatenate([high.T, high.T, low.T], axis=1))
        j = np.arange(SIDE)
        p2 = np.arange(SIDE)
        steps = (2 * p1[:, None] + offset + 128 * p2[None, :])[:, :, None] * j
        angle = (steps % 8192) * (2.0 * np.pi / 8192)
        stage = np.stack([np.cos(angle), -np.sin(angle)], axis=-1).reshape(SIDE, SIDE, 2 * SIDE)
        high, low = split_np(stage)
        second.append(np.concatenate([high, high, low], axis=2))
        high, low = (np.swapaxes(part, 1, 2) for part in (high, low))
        second_t.append(np.concatenate([high, high, low], axis=2))
    return [np.stack(tables) for tables in (first, first_t, second, second_t)]


def split(values):
    high = values.astype(BF16)
    low = (values - high.astype(F32)).astype(BF16)
    return high, low


def place(order):
    return 2 * lax.shift_right_logical(order, 6) + lax.bitwise_and(order, 1)


def narrow(in_re, in_im, out_ref):
    count, rows, width = out_ref.shape

    def step(k, _):
        for source, low in ((in_re, 0), (in_im, width // 2)):
            values = [
                source[pl.ds((k * GROUP + e) * PITCH, rows), :].astype(BF16) for e in range(GROUP)
            ]
            for e in range(GROUP):
                out_ref[k * GROUP + e, :, low : low + width // 2] = values[e]
        return 0

    lax.fori_loop(0, count // GROUP, step, 0)


def synth_kernel(meta, nodes, coeffs_ref, alpha_ref, beta_ref, leg_ref, out_ref, filters, acc_re, acc_im):
    slots, cycles, degrees = leg_ref.shape
    radii = nodes.shape[0]

    def fill(r, _):
        filters[pl.ds(r, 1), :] = alpha_ref[pl.ds(nodes[r], 1), :]
        filters[pl.ds(radii + r, 1), :] = beta_ref[pl.ds(nodes[r], 1), :]
        return 0

    lax.fori_loop(0, radii, fill, 0, unroll=8)
    degree = meta[0] + lax.broadcasted_iota(jnp.int32, (1, degrees), 1)

    def step(k, _):
        results = []
        for e in range(GROUP):
            s = k * GROUP + e
            order = meta[1 + s]
            live = degree >= order
            parts = []
            for c in range(2):
                row = jnp.where(live, coeffs_ref[c, pl.ds(s, 1), :], 0.0)
                parts.append((filters[...] * row).astype(BF16))
            filtered = jnp.concatenate(parts, axis=0)
            harmonic = lax.dot_general(
                leg_ref[s], filtered, (((1,), (1,)), ((), ())), preferred_element_type=F32
            )
            results.append((pl.ds(place(order), cycles, stride=PITCH), harmonic))
        for at, harmonic in results:
            acc_re[at, :] = harmonic[:, : 2 * radii]
            acc_im[at, :] = harmonic[:, 2 * radii :]
        return 0

    lax.fori_loop(0, slots // GROUP, step, 0)
    narrow(acc_re, acc_im, out_ref)


def cycle_kernel(
    offset, parts_ref, place_ref, weight_ref, first_ref, first_t_ref, second_ref, second_t_ref,
    out_ref, sum_re, sum_im, spectra, middle, products, middle_t, back_re, back_im,
):
    owners, slots, width = out_ref.shape
    half = width // 2
    few = slots // 2

    def gather(k, _):
        loaded = []
        for e in range(4):
            a = k * 4 + e
            low = parts_ref[a, :few].astype(F32) + parts_ref[a, few : 2 * few].astype(F32)
            loaded.append((a, low, parts_ref[a, 2 * few :].astype(F32)))
        for a, low, high in loaded:
            for start, values in ((0, low), (few, high)):
                rows = pl.ds(a * PITCH + start, few)
                sum_re[rows, :] = values[:, :half]
                sum_im[rows, :] = values[:, half:]
        return 0

    lax.fori_loop(0, owners // 4, gather, 0)
    row_j = lax.broadcasted_iota(jnp.int32, (SIDE, 2 * SIDE), 0)

    def sort(k, _):
        results = []
        for e in range(4):
            b = k * 4 + e
            pick = row_j == place_ref[pl.ds(b, 1), :]
            one = jnp.where((row_j == 0) & (b == 0), 0.5, 1.0)
            table = jnp.where(pick, one, 0.0).astype(BF16)
            terms = []
            for source in (sum_re, sum_im):
                values = jnp.concatenate(
                    [source[pl.ds(2 * b + h, owners, stride=PITCH), :] for h in range(2)], axis=0
                )
                terms.append(jnp.concatenate(split(values), axis=0))
            terms = jnp.concatenate(terms, axis=1)
            results.append((b, jnp.dot(table, terms, preferred_element_type=F32)))
        for b, placed in results:
            spectra[pl.ds(b, SIDE, stride=PITCH), :] = placed[:, :half]
            spectra[pl.ds(BLOCKS + b, SIDE, stride=PITCH), :] = placed[:, half:]
        return 0

    lax.fori_loop(0, BLOCKS // 4, sort, 0)

    def synth_first(k, _):
        results = []
        for i in range(4):
            pair = []
            for e in range(2):
                j = (4 * k + i) * 2 + e
                high, low = split(spectra[pl.ds(j * PITCH, SIDE), :])
                pair.append(jnp.concatenate([high, low, high], axis=0))
            results.append(
                jnp.dot(first_ref[0], jnp.concatenate(pair, axis=1), preferred_element_type=F32)
            )
        for i in range(4):
            for e in range(2):
                j = (4 * k + i) * 2 + e
                for c in range(2):
                    middle[pl.ds((2 * j + c) * PITCH, SIDE), :] = results[i][
                        c * SIDE : (c + 1) * SIDE, e * half : (e + 1) * half
                    ]
        return 0

    lax.fori_loop(0, SIDE // 8, synth_first, 0)
    lower = lax.broadcasted_iota(jnp.int32, (SIDE, half), 1) < half // 2

    def synth_second(k, total):
        results = []
        for e in range(4):
            p1 = 4 * k + e
            high, low = split(middle[pl.ds(p1, 2 * SIDE, stride=PITCH), :])
            values = jnp.concatenate([high, low, high], axis=0)
            fields = jnp.dot(second_ref[0, p1], values, preferred_element_type=F32)
            swapped = pltpu.roll(fields, half // 2, 1)
            product = swapped * jnp.where(lower, swapped, fields)
            total = total + product
            results.append(product)
        for e in range(4):
            products[4 * k + e] = results[e]
        return total

    total = lax.fori_loop(0, SIDE // 4, synth_second, jnp.zeros((SIDE, half), F32))
    mean = jnp.sum(total, axis=0, keepdims=True) * (1.0 / NPIX)

    def analyse_second(k, _):
        results = []
        for e in range(4):
            p1 = 4 * k + e
            high, low = split(products[p1] - mean)
            values = jnp.concatenate([high, low, high], axis=0)
            results.append(jnp.dot(second_t_ref[0, p1], values, preferred_element_type=F32))
        for e in range(4):
            middle_t[pl.ds(4 * k + e, 2 * SIDE, stride=PITCH), :] = results[e]
        return 0

    lax.fori_loop(0, SIDE // 4, analyse_second, 0)
    scale = weight_ref[0] * 0.5

    def analyse_first(k, _):
        results = []
        for i in range(4):
            pair = []
            for e in range(2):
                j = (4 * k + i) * 2 + e
                values = jnp.concatenate(
                    [middle_t[pl.ds((2 * j + c) * PITCH, SIDE), :] for c in range(2)], axis=0
                )
                high, low = split(values)
                pair.append(jnp.concatenate([high, low, high], axis=0))
            results.append(
                jnp.dot(first_t_ref[0], jnp.concatenate(pair, axis=1), preferred_element_type=F32)
            )
        for i in range(4):
            for e in range(2):
                j = (4 * k + i) * 2 + e
                spectra[pl.ds(j * PITCH, SIDE), :] = results[i][:, e * half : (e + 1) * half] * scale
        return 0

    lax.fori_loop(0, SIDE // 8, analyse_first, 0)

    def unsort(k, _):
        results = []
        for e in range(4):
            b = 4 * k + e
            pick = row_j == place_ref[pl.ds(b, 1), :]
            table = jnp.where(pick, 1.0, 0.0)[:, :SIDE].astype(BF16)
            values = jnp.concatenate(
                [
                    spectra[pl.ds(c * BLOCKS + b, SIDE, stride=PITCH), :].astype(BF16)
                    for c in range(2)
                ],
                axis=1,
            )
            results.append(
                lax.dot_general(
                    table, values, (((0,), (0,)), ((), ())), preferred_element_type=F32
                )
            )
        for e in range(4):
            for h in range(2):
                at = pl.ds(2 * (4 * k + e) + h, owners, stride=PITCH)
                back_re[at, :] = results[e][h * owners : (h + 1) * owners, :half]
                back_im[at, :] = results[e][h * owners : (h + 1) * owners, half:]
        return 0

    lax.fori_loop(0, BLOCKS // 4, unsort, 0)
    narrow(back_re, back_im, out_ref)


def adjoint_kernel(
    meta, nodes, radial, alpha_ref, beta_ref, leg_ref, parts_ref, out_ref, filters, weights, in_re, in_im
):
    slots, cycles, degrees = leg_ref.shape
    radii = nodes.shape[0]

    def fill(r, _):
        node = nodes[r]
        filters[pl.ds(r, 1), :] = alpha_ref[pl.ds(node, 1), :] * radial[node]
        filters[pl.ds(radii + r, 1), :] = beta_ref[pl.ds(node, 1), :] * (2.0 * radial[node])
        return 0

    lax.fori_loop(0, radii, fill, 0, unroll=8)
    high, low = split(filters[...])
    weights[: 2 * radii, :] = high
    weights[2 * radii :, :] = low
    degree = meta[0] + lax.broadcasted_iota(jnp.int32, (1, degrees), 1)

    def widen(k, _):
        for target, low in ((in_re, 0), (in_im, 2 * radii)):
            values = [
                parts_ref[k * GROUP + e, :, low : low + 2 * radii].astype(F32) for e in range(GROUP)
            ]
            for e in range(GROUP):
                target[pl.ds((k * GROUP + e) * PITCH, slots), :] = values[e]
        return 0

    lax.fori_loop(0, cycles // GROUP, widen, 0)

    def step(k, _):
        results = []
        for e in range(4):
            s = k * 4 + e
            order = meta[1 + s]
            live = degree >= order
            at = pl.ds(place(order), cycles, stride=PITCH)
            legendre = leg_ref[s].astype(F32)
            for c, source in enumerate((in_re, in_im)):
                values = source[at, :].astype(BF16)
                values = jnp.concatenate([values, values], axis=1)
                summed = jnp.dot(values, weights[...], preferred_element_type=F32)
                row = jnp.sum(summed * legendre, axis=0, keepdims=True)
                results.append((c, s, jnp.where(live, row, 0.0)))
        for c, s, row in results:
            out_ref[c, pl.ds(s, 1), :] = row
        return 0

    lax.fori_loop(0, slots // 4, step, 0)


MESH_IDS = pl.DeviceIdType.MESH
CHIPS = 64
BATCH = 8


def around(i, sign=1):
    row, ma = lax.axis_index("row"), lax.axis_index("ma")
    shift = (i * 27) % CHIPS
    x = ((ma // 4) % 4 + sign * (shift % 4) + 4) % 4
    z = (ma % 4 + sign * ((shift // 4) % 4) + 4) % 4
    y = ((ma // 16) * 2 + row // 2 + sign * (shift // 16) + 4) % 4
    return y % 2, (y // 2 * 4 + x) * 4 + z


def greet():
    row, ma = lax.axis_index("row"), lax.axis_index("ma")
    core = row % 2
    barrier = pltpu.get_barrier_semaphore()
    sibling = (row + 1 - 2 * core, ma)
    pl.semaphore_signal(barrier, inc=1, device_id=sibling, device_id_type=MESH_IDS)

    def signal(i, _):
        y_lo, owner = around(i)
        pl.semaphore_signal(
            barrier, inc=1, device_id=(y_lo * 2 + core, owner), device_id_type=MESH_IDS
        )
        return 0

    lax.fori_loop(1, CHIPS, signal, 0)
    pl.semaphore_wait(barrier, CHIPS)
    return row // 2, core, ma, sibling


def spread_kernel(src, out, other, total, pair_send, pair_recv, send, recv):
    slots = src.shape[2]
    y_here, core, ma, sibling = greet()

    for side in range(2):
        live = slots * (side + 1) // 2
        start = side * slots // 2

        @pl.when(y_here == side)
        def _():
            def swap(i, _):
                y_lo, owner = around(i)
                pltpu.make_async_remote_copy(
                    src_ref=src.at[owner * 2 + y_lo, 1 - core, pl.ds(0, live)],
                    dst_ref=other.at[i, pl.ds(0, live)],
                    send_sem=pair_send,
                    recv_sem=pair_recv.at[i // BATCH],
                    device_id=sibling,
                    device_id_type=MESH_IDS,
                ).start()
                return 0

            lax.fori_loop(0, CHIPS, swap, 0)

            def add(i):
                y_lo, owner = around(i)
                mine = src[owner * 2 + y_lo, core, :live].astype(F32)
                total[i, :live] = (mine + other[i, :live].astype(F32)).astype(BF16)
                return y_lo, owner

            def post(i, _):
                y_lo, owner = add(i)
                pltpu.make_async_remote_copy(
                    src_ref=total.at[i, pl.ds(0, live)],
                    dst_ref=out.at[ma, pl.ds(start, live)],
                    send_sem=send,
                    recv_sem=recv,
                    device_id=(y_lo * 2 + core, owner),
                    device_id_type=MESH_IDS,
                ).start()
                return 0

            def chunk(k, _):
                here = other.at[pl.ds(k * BATCH, BATCH), pl.ds(0, live)]
                pltpu.make_async_copy(here, here, pair_recv.at[k]).wait()

                @pl.when(k == 0)
                def _():
                    add(0)
                    pltpu.make_async_copy(
                        total.at[0, pl.ds(0, live)], out.at[ma, pl.ds(start, live)], recv
                    ).start()

                lax.fori_loop(jnp.where(k == 0, 1, k * BATCH), (k + 1) * BATCH, post, 0)
                return 0

            lax.fori_loop(0, CHIPS // BATCH, chunk, 0)
            sent = other.at[:, pl.ds(0, live)]
            pltpu.make_async_copy(sent, sent, pair_send).wait()
            sent = total.at[pl.ds(0, CHIPS - 1), pl.ds(0, live)]
            pltpu.make_async_copy(sent, sent, send).wait()

    pltpu.make_async_copy(out, out, recv).wait()


def return_kernel(src, out, pair_send, pair_recv, send, recv):
    slots = src.shape[1]
    y_here, core, ma, sibling = greet()
    chip = ma * 2 + y_here
    for side in range(2):
        live = slots * (side + 1) // 2

        @pl.when(y_here == side)
        def _():
            pltpu.make_async_copy(
                src.at[ma, pl.ds(0, live)], out.at[chip, core, pl.ds(0, live)], recv.at[0]
            ).start()

    def post(i, _):
        y_lo, owner = around(i)
        for side in range(2):
            live = slots * (side + 1) // 2

            @pl.when(y_lo == side)
            def _():
                pltpu.make_async_remote_copy(
                    src_ref=src.at[owner, pl.ds(0, live)],
                    dst_ref=out.at[chip, core, pl.ds(0, live)],
                    send_sem=send.at[side],
                    recv_sem=recv.at[i // BATCH],
                    device_id=(side * 2 + core, owner),
                    device_id_type=MESH_IDS,
                ).start()

        return 0

    lax.fori_loop(1, CHIPS, post, 0)
    for side in range(2):
        live = slots * (side + 1) // 2

        @pl.when(y_here == side)
        def _():
            def chunk(k, _):
                here = out.at[pl.ds(0, BATCH), 0, pl.ds(0, live)]
                pltpu.make_async_copy(here, here, recv.at[k]).wait()

                def forward(i, _):
                    y_lo, owner = around(i, -1)
                    piece = out.at[owner * 2 + y_lo, core, pl.ds(0, live)]
                    pltpu.make_async_remote_copy(
                        src_ref=piece,
                        dst_ref=piece,
                        send_sem=pair_send,
                        recv_sem=pair_recv,
                        device_id=sibling,
                        device_id_type=MESH_IDS,
                    ).start()
                    return 0

                lax.fori_loop(k * BATCH, (k + 1) * BATCH, forward, 0)
                return 0

            lax.fori_loop(0, CHIPS // BATCH, chunk, 0)
            half = out.at[:, 0, pl.ds(0, live)]
            pltpu.make_async_copy(half, half, pair_send).wait()
            pltpu.make_async_copy(half, half, pair_recv).wait()
            for to in range(2):
                count = CHIPS // 2 - (1 if to == side else 0)
                sent = src.at[pl.ds(0, count), pl.ds(0, slots * (to + 1) // 2)]
                pltpu.make_async_copy(sent, sent, send.at[to]).wait()


VMEM = pl.BlockSpec(memory_space=pltpu.VMEM)
SMEM = pl.BlockSpec(memory_space=pltpu.SMEM)


def params(mib):
    return pltpu.CompilerParams(vmem_limit_bytes=mib * 2**20)


def remote_params(collective_id):
    return pltpu.CompilerParams(
        collective_id=collective_id, has_side_effects=True, vmem_limit_bytes=40 * 2**20
    )


def body(
    coeffs, legendre, alpha_table, beta_table, radial_weight, radius_index, orders, cycle_offset, cycle_weight
):
    row_id = lax.axis_index("row")
    ma_id = lax.axis_index("ma")
    ma_count = lax.axis_size("ma")
    slots, cycles, degrees = legendre.shape
    radii = radius_index.shape[0]
    width = 4 * radii
    my_orders = lax.dynamic_slice_in_dim(orders, ma_id * slots, slots)
    meta = jnp.concatenate([jnp.full((1,), row_id * degrees, jnp.int32), my_orders])
    own = (row_id,)
    offset = lax.dynamic_slice(cycle_offset, own, (1,))
    weight = lax.dynamic_slice(cycle_weight, own, (1,))

    of_owner = orders.reshape(ma_count, 1, slots)
    where = place(of_owner) == jnp.arange(slots, dtype=jnp.int32)[None, :, None]
    placed = jnp.sum(jnp.where(where, lax.bitwise_and(of_owner, SIDE - 1), 0), axis=2)
    placed = jnp.transpose(placed.reshape(ma_count, BLOCKS, 2), (1, 2, 0)).reshape(BLOCKS, SIDE)
    placed = jnp.concatenate([placed, placed], axis=1)

    harmonic = pl.pallas_call(
        synth_kernel,
        out_shape=jax.ShapeDtypeStruct((cycles, slots, width), BF16),
        in_specs=[SMEM, SMEM, VMEM, VMEM, VMEM, VMEM],
        out_specs=VMEM,
        scratch_shapes=[
            pltpu.VMEM((2 * radii, degrees), F32),
            pltpu.VMEM((cycles * PITCH, 2 * radii), F32),
            pltpu.VMEM((cycles * PITCH, 2 * radii), F32),
        ],
        compiler_params=params(56),
        name="synth",
    )(meta, radius_index, coeffs, alpha_table, beta_table, legendre)

    chips = cycles // 2
    batches = chips // BATCH
    parts = pl.pallas_call(
        spread_kernel,
        out_shape=jax.ShapeDtypeStruct((ma_count, slots + slots // 2, width), BF16),
        in_specs=[VMEM],
        out_specs=VMEM,
        scratch_shapes=[
            pltpu.VMEM((chips, slots, width), BF16),
            pltpu.VMEM((chips, slots, width), BF16),
            pltpu.SemaphoreType.DMA,
            pltpu.SemaphoreType.DMA((batches,)),
            pltpu.SemaphoreType.DMA,
            pltpu.SemaphoreType.DMA,
        ],
        compiler_params=remote_params(1),
        name="spread",
    )(harmonic.reshape(chips, 2, slots, width))

    tables = [jnp.asarray(table) for table in dft_tables()]
    whole = lambda *shape: pl.BlockSpec(shape, lambda i, off: (0,) * len(shape))
    chosen = lambda table: pl.BlockSpec(
        (1,) + table.shape[1:], lambda i, off: (off[0],) + (0,) * (table.ndim - 1)
    )
    plane = lambda groups: pltpu.VMEM((groups * PITCH, 2 * radii), F32)
    analysed = pl.pallas_call(
        cycle_kernel,
        out_shape=jax.ShapeDtypeStruct((ma_count, slots, width), BF16),
        grid_spec=pltpu.PrefetchScalarGridSpec(
            num_scalar_prefetch=1,
            grid=(1,),
            in_specs=[
                whole(*parts.shape),
                whole(*placed.shape),
                pl.BlockSpec(memory_space=pltpu.SMEM),
                *[chosen(table) for table in tables],
            ],
            out_specs=whole(ma_count, slots, width),
            scratch_shapes=[
                plane(ma_count),
                plane(ma_count),
                plane(SIDE),
                plane(2 * SIDE),
                pltpu.VMEM((SIDE, SIDE, 2 * radii), F32),
                plane(2 * SIDE),
                plane(ma_count),
                plane(ma_count),
            ],
        ),
        compiler_params=params(60),
        name="cycle",
    )(offset, parts, placed, weight, *tables)

    returned = pl.pallas_call(
        return_kernel,
        out_shape=jax.ShapeDtypeStruct((chips, 2, slots, width), BF16),
        in_specs=[VMEM],
        out_specs=VMEM,
        scratch_shapes=[
            pltpu.SemaphoreType.DMA,
            pltpu.SemaphoreType.DMA,
            pltpu.SemaphoreType.DMA((2,)),
            pltpu.SemaphoreType.DMA((batches,)),
        ],
        compiler_params=remote_params(2),
        name="return",
    )(analysed)
    returned = returned.reshape(cycles, slots, width)

    return pl.pallas_call(
        adjoint_kernel,
        out_shape=jax.ShapeDtypeStruct((2, slots, degrees), F32),
        in_specs=[SMEM, SMEM, SMEM, VMEM, VMEM, VMEM, VMEM],
        out_specs=VMEM,
        scratch_shapes=[
            pltpu.VMEM((2 * radii, degrees), F32),
            pltpu.VMEM((4 * radii, degrees), BF16),
            pltpu.VMEM((cycles * PITCH, 2 * radii), F32),
            pltpu.VMEM((cycles * PITCH, 2 * radii), F32),
        ],
        compiler_params=params(56),
        name="adjoint",
    )(meta, radius_index, radial_weight, alpha_table, beta_table, legendre, returned)


def solution(mesh):
    in_specs = (
        P(None, "ma", "row"),
        P("ma", None, "row"),
        P(None, "row"),
        P(None, "row"),
        P(),
        P(),
        P(),
        P("ma"),
        P("ma"),
    )
    return jax.shard_map(
        body, mesh=mesh, in_specs=in_specs, out_specs=P(None, "ma", "row"), check_vma=False
    )
```

time: 219 us -> 132 us (0.60)
  blocking collectives: 61.4 us -> 0 us
  waiting for transfers between devices: 50.8 us -> 0 us
  Pallas kernels: 83.1 us -> 121 us
  starting transfers between devices: 11.1 us -> 0 us
    pallas_call x0 -> x2, Pallas kernels: none -> 71.6 us  [the longest x1 36 us: body(): pl.pallas_call(return_kernel, out_shape=jax.ShapeDtypeStruct((chips, 2, s...]
    all_to_all x1 -> x0, blocking collectives: 61.4 us -> none  [body(): lax.all_to_all(spread, both, split_axis=0, concat_axis=0, tiled=True)]
    all_to_all x1 -> x0, waiting for transfers between devices: 50.8 us -> none  [body(): lax.all_to_all(harmonic, both, split_axis=0, concat_axis=0, tiled=True)]
    pallas_call x1, Pallas kernels: 41.3 us -> 21.7 us  [body(): pl.pallas_call(cycle_kernel, out_shape=jax.ShapeDtypeStruct((ma_count, sl...]
    all_to_all x1 -> x0, starting transfers between devices: 11.1 us -> none  [body(): lax.all_to_all(harmonic, both, split_axis=0, concat_axis=0, tiled=True)]
    pallas_call x1, Pallas kernels: 21.6 us -> 13.5 us  [body(): pl.pallas_call(synth_kernel, out_shape=jax.ShapeDtypeStruct((cycles, slot...]
    pallas_call x1, Pallas kernels: 20.1 us -> 13.9 us  [body(): pl.pallas_call(adjoint_kernel, out_shape=jax.ShapeDtypeStruct((2, slots,...]
    unnamed x24 -> x14, local copies, waits for them, and re-layouts: 5.4 us -> 6.5 us
  transfers between devices with their start and end apart: 1 -> 0, of which waited for: 1 -> 0; matrix products, arithmetic and copies ran while one was open for 1% -> 0% of each run, Pallas kernels for 0% -> 0%
where the time goes in v2:
time: 132 us
  Pallas kernels  121 us (92%)
  local copies, waits for them, and re-layouts  8.88 us (7%)
  other arithmetic  1.93 us (1%)
    pallas_call x1, Pallas kernels, body(): pl.pallas_call(return_kernel, out_shape=jax.ShapeDtypeStruct((chips, 2, s...  36 us
    pallas_call x1, Pallas kernels, body(): pl.pallas_call(spread_kernel, out_shape=jax.ShapeDtypeStruct((ma_count, s...  35.6 us
    pallas_call x1, Pallas kernels, body(): pl.pallas_call(cycle_kernel, out_shape=jax.ShapeDtypeStruct((ma_count, sl...  21.7 us
    pallas_call x1, Pallas kernels, body(): pl.pallas_call(adjoint_kernel, out_shape=jax.ShapeDtypeStruct((2, slots,...  13.9 us
    pallas_call x1, Pallas kernels, body(): pl.pallas_call(synth_kernel, out_shape=jax.ShapeDtypeStruct((cycles, slot...  13.5 us
    unnamed x14, local copies, waits for them, and re-layouts  6.5 us

profile of v2, /device:TPU:15, one launch (start us, length us, event | category | flops | bytes accessed | tf_op | source)
XLA Modules:
  0.0 131.5 jit_solution(6549082507600698130)
XLA Ops:
  0.0 0.8 dynamic_slice.9
  0.8 0.6 pad_add_fusion.1.meta
  1.4 0.0 copy-start.5
  1.4 0.0 copy-start.6
  1.4 0.0 copy-start.4
  1.4 13.5 %synth.1 = bf16[128,64,256]{2,1,0:T(8,128)(2,1)} custom-call(s32[65]{0:T(128)} %pad_add_fusion.1.meta, s32[64]{0:T(128)} %nodes.3, f32[2,64,512]{2,1,0:T(8,128)} %coeffs_ref.1, f32[64,512]{1,0:T(8,128)} %alpha_ref.3, f32[64,512]{1,0:T(8,128)} %beta_ref.3, bf16[64,128,512]{2,1,0:T(8,128)(2,1)} %leg_ref.3), custom_call_target="tpu_custom_call" | custom-call | tf_op jit(solution)/shard_map/synth/pallas_call | solution.py:513
  14.8 0.0 copy-start
  14.8 2.2 %copy-done = bf16[128,64,256]{2,1,0:T(8,128)(2,1)S(1)} copy-done((bf16[128,64,256]{2,1,0:T(8,128)(2,1)S(1)}, bf16[128,64,256]{2,1,0:T(8,128)(2,1)}, u32[]{:S(2)}) %copy-start) | copy-done | bytes 4194328
  17.0 35.6 %spread.1.parts_ref = bf16[32,96,256]{2,1,0:T(8,128)(2,1)S(1)} custom-call(bf16[64,2,64,256]{3,2,1,0:T(8,128)(2,1)S(1)} %bitcast.6), custom_call_target="tpu_custom_call" | custom-call | tf_op jit(solution)/shard_map/spread/pallas_call | solution.py:529
  52.7 0.0 copy-start.2
  52.7 1.1 copy-done.2
  53.8 0.0 copy-done.5
  53.8 0.6 dynamic_slice.10.offset
  54.5 0.0 copy-done.6
  54.5 0.7 dynamic_slice.11.weight_ref
  55.2 0.0 copy-done.4
  55.2 0.1 add.21
  55.2 0.1 and.32
  55.3 0.6 select_reduce_fusion
  55.9 0.1 copy.15
  56.0 0.1 reshape.49
  56.1 0.7 pad_add_fusion.place_ref
  56.8 21.7 %cycle.1.src = bf16[32,64,256]{2,1,0:T(8,128)(2,1)} custom-call(s32[1]{0:T(128)} %dynamic_slice.10.offset, bf16[32,96,256]{2,1,0:T(8,128)(2,1)} %copy-done.2, s32[32,128]{1,0:T(8,128)} %pad_add_fusion.place_ref, f32[1]{0:T(128)} %dynamic_slice.11.weight_ref, bf16[2,128,192]{2,1,0:T(8,128)(2,1)} %constant.35.clone.first_ref, ...), custom_call_target="tpu_custom_call" | custom-call | tf_op jit(solution)/shard_map/cycle/pallas_call | solution.py:552
  78.4 0.0 copy-start.3
  78.5 1.2 copy-done.3
  79.7 36.0 %return.1 = bf16[64,2,64,256]{3,2,1,0:T(8,128)(2,1)S(1)} custom-call(bf16[32,64,256]{2,1,0:T(8,128)(2,1)S(1)} %copy-done.3), custom_call_target="tpu_custom_call" | custom-call | tf_op jit(solution)/shard_map/return/pallas_call | solution.py:580
  115.7 0.0 copy-start.1
  115.7 1.9 %copy-done.1 = bf16[64,2,64,256]{3,2,1,0:T(8,128)(2,1)} copy-done((bf16[64,2,64,256]{3,2,1,0:T(8,128)(2,1)}, bf16[64,2,64,256]{3,2,1,0:T(8,128)(2,1)S(1)}, u32[]{:S(2)}) %copy-start.1) | copy-done | bytes 4194328
  117.6 13.9 %adjoint.1 = f32[2,64,512]{2,1,0:T(8,128)} custom-call(s32[65]{0:T(128)} %pad_add_fusion.1.meta, s32[64]{0:T(128)} %nodes.3, f32[64]{0:T(128)} %radial.1, f32[64,512]{1,0:T(8,128)} %alpha_ref.3, f32[64,512]{1,0:T(8,128)} %beta_ref.3, bf16[64,128,512]{2,1,0:T(8,128)(2,1)} %leg_ref.3, bf16[128,64,256]{2,1,0:T(8,128)(2,1)} %bitcast.7), custom_call_target="tpu_custom_call" | custom-call | tf_op jit(solution)/shard_map/adjoint/pallas_call | solution.py:596
  (1 shorter events, 0.0 us)
Async XLA Ops:
  1.4 52.5 %copy-start.5 = (s32[4]{0:T(128)S(1)}, s32[4]{0:T(128)}, u32[]{:S(2)}) copy-start(s32[4]{0:T(128)} %param.20) | copy-start | bytes 52
  1.4 53.1 %copy-start.6 = (f32[4]{0:T(128)S(1)}, f32[4]{0:T(128)}, u32[]{:S(2)}) copy-start(f32[4]{0:T(128)} %param.21) | copy-start | bytes 52
  1.4 53.8 %copy-start.4 = (s32[2048]{0:T(1024)S(1)}, s32[2048]{0:T(1024)}, u32[]{:S(2)}) copy-start(s32[2048]{0:T(1024)} %param.19) | copy-start | bytes 24580
  14.8 2.2 %copy-start = (bf16[128,64,256]{2,1,0:T(8,128)(2,1)S(1)}, bf16[128,64,256]{2,1,0:T(8,128)(2,1)}, u32[]{:S(2)}) copy-start(bf16[128,64,256]{2,1,0:T(8,128)(2,1)} %synth.1) | copy-start | bytes 12582916
  52.7 1.2 copy-start.2
  78.4 1.2 copy-start.3
  115.7 1.9 %copy-start.1 = (bf16[64,2,64,256]{3,2,1,0:T(8,128)(2,1)}, bf16[64,2,64,256]{3,2,1,0:T(8,128)(2,1)S(1)}, u32[]{:S(2)}) copy-start(bf16[64,2,64,256]{3,2,1,0:T(8,128)(2,1)S(1)} %return.1) | copy-start | bytes 12582916

commit v3 on v2

v3 whole, which is shorter than its diff:
```python
import functools

import jax
import jax.numpy as jnp
import ml_dtypes
import numpy as np
from jax import lax
from jax.experimental import pallas as pl
from jax.experimental.pallas import tpu as pltpu
from jax.sharding import PartitionSpec as P

NPIX = 4096
SIDE = 64
BLOCKS = 32
PITCH = 65
GROUP = 8
ROUND = 32
BF16 = jnp.bfloat16
F32 = jnp.float32


def split_np(table):
    high = table.astype(ml_dtypes.bfloat16)
    low = (table - high.astype(np.float64)).astype(ml_dtypes.bfloat16)
    return high, low


def dft_tables():
    p1 = np.arange(SIDE)
    first, first_t, second, second_t = [], [], [], []
    for offset in (0, 1):
        b = np.arange(BLOCKS)
        angle = (np.outer(2 * p1 + offset, b) % 128) * (2.0 * np.pi / 128)
        cos, sin = 2.0 * np.cos(angle), 2.0 * np.sin(angle)
        stage = np.block([[cos, -sin], [sin, cos]])
        high, low = split_np(stage)
        first.append(np.concatenate([high, high, low], axis=1))
        first_t.append(np.concatenate([high.T, high.T, low.T], axis=1))
        j = np.arange(SIDE)
        p2 = np.arange(SIDE)
        steps = (2 * p1[:, None] + offset + 128 * p2[None, :])[:, :, None] * j
        angle = (steps % 8192) * (2.0 * np.pi / 8192)
        stage = np.stack([np.cos(angle), -np.sin(angle)], axis=-1).reshape(SIDE, SIDE, 2 * SIDE)
        high, low = split_np(stage)
        second.append(np.concatenate([high, high, low], axis=2))
        high, low = (np.swapaxes(part, 1, 2) for part in (high, low))
        second_t.append(np.concatenate([high, high, low], axis=2))
    return [np.stack(tables) for tables in (first, first_t, second, second_t)]


def split(values):
    high = values.astype(BF16)
    low = (values - high.astype(F32)).astype(BF16)
    return high, low


def place(order):
    return 2 * lax.shift_right_logical(order, 6) + lax.bitwise_and(order, 1)


def narrow(in_re, in_im, pitch, store):
    count, half = in_re.shape[0] // pitch, in_re.shape[1]

    def step(k, _):
        for source, low in ((in_re, 0), (in_im, half)):
            values = [
                source[pl.ds((k * GROUP + e) * pitch, pitch - 1), :].astype(BF16)
                for e in range(GROUP)
            ]
            for e in range(GROUP):
                store(k * GROUP + e, low, values[e])
        return 0

    lax.fori_loop(0, count // GROUP, step, 0)


def cycle_kernel(
    offset, parts_ref, place_ref, weight_ref, first_ref, first_t_ref, second_ref, second_t_ref,
    out_ref, sum_re, sum_im, spectra, middle, products, middle_t, back_re, back_im,
):
    owners, slots, width = out_ref.shape
    half = width // 2
    few = slots // 2

    def gather(k, _):
        loaded = []
        for e in range(4):
            a = k * 4 + e
            low = parts_ref[a, :few].astype(F32) + parts_ref[a, few : 2 * few].astype(F32)
            loaded.append((a, low, parts_ref[a, 2 * few :].astype(F32)))
        for a, low, high in loaded:
            for start, values in ((0, low), (few, high)):
                rows = pl.ds(a * PITCH + start, few)
                sum_re[rows, :] = values[:, :half]
                sum_im[rows, :] = values[:, half:]
        return 0

    lax.fori_loop(0, owners // 4, gather, 0)
    row_j = lax.broadcasted_iota(jnp.int32, (SIDE, 2 * SIDE), 0)

    def sort(k, _):
        results = []
        for e in range(4):
            b = k * 4 + e
            pick = row_j == place_ref[pl.ds(b, 1), :]
            one = jnp.where((row_j == 0) & (b == 0), 0.5, 1.0)
            table = jnp.where(pick, one, 0.0).astype(BF16)
            terms = []
            for source in (sum_re, sum_im):
                values = jnp.concatenate(
                    [source[pl.ds(2 * b + h, owners, stride=PITCH), :] for h in range(2)], axis=0
                )
                terms.append(jnp.concatenate(split(values), axis=0))
            terms = jnp.concatenate(terms, axis=1)
            results.append((b, jnp.dot(table, terms, preferred_element_type=F32)))
        for b, placed in results:
            spectra[pl.ds(b, SIDE, stride=PITCH), :] = placed[:, :half]
            spectra[pl.ds(BLOCKS + b, SIDE, stride=PITCH), :] = placed[:, half:]
        return 0

    lax.fori_loop(0, BLOCKS // 4, sort, 0)

    def synth_first(k, _):
        results = []
        for i in range(4):
            pair = []
            for e in range(2):
                j = (4 * k + i) * 2 + e
                high, low = split(spectra[pl.ds(j * PITCH, SIDE), :])
                pair.append(jnp.concatenate([high, low, high], axis=0))
            results.append(
                jnp.dot(first_ref[0], jnp.concatenate(pair, axis=1), preferred_element_type=F32)
            )
        for i in range(4):
            for e in range(2):
                j = (4 * k + i) * 2 + e
                for c in range(2):
                    middle[pl.ds((2 * j + c) * PITCH, SIDE), :] = results[i][
                        c * SIDE : (c + 1) * SIDE, e * half : (e + 1) * half
                    ]
        return 0

    lax.fori_loop(0, SIDE // 8, synth_first, 0)
    lower = lax.broadcasted_iota(jnp.int32, (SIDE, half), 1) < half // 2

    def synth_second(k, total):
        results = []
        for e in range(4):
            p1 = 4 * k + e
            high, low = split(middle[pl.ds(p1, 2 * SIDE, stride=PITCH), :])
            values = jnp.concatenate([high, low, high], axis=0)
            fields = jnp.dot(second_ref[0, p1], values, preferred_element_type=F32)
            swapped = pltpu.roll(fields, half // 2, 1)
            product = swapped * jnp.where(lower, swapped, fields)
            total = total + product
            results.append(product)
        for e in range(4):
            products[4 * k + e] = results[e]
        return total

    total = lax.fori_loop(0, SIDE // 4, synth_second, jnp.zeros((SIDE, half), F32))
    mean = jnp.sum(total, axis=0, keepdims=True) * (1.0 / NPIX)

    def analyse_second(k, _):
        results = []
        for e in range(4):
            p1 = 4 * k + e
            high, low = split(products[p1] - mean)
            values = jnp.concatenate([high, low, high], axis=0)
            results.append(jnp.dot(second_t_ref[0, p1], values, preferred_element_type=F32))
        for e in range(4):
            middle_t[pl.ds(4 * k + e, 2 * SIDE, stride=PITCH), :] = results[e]
        return 0

    lax.fori_loop(0, SIDE // 4, analyse_second, 0)
    scale = weight_ref[0] * 0.5

    def analyse_first(k, _):
        results = []
        for i in range(4):
            pair = []
            for e in range(2):
                j = (4 * k + i) * 2 + e
                values = jnp.concatenate(
                    [middle_t[pl.ds((2 * j + c) * PITCH, SIDE), :] for c in range(2)], axis=0
                )
                high, low = split(values)
                pair.append(jnp.concatenate([high, low, high], axis=0))
            results.append(
                jnp.dot(first_t_ref[0], jnp.concatenate(pair, axis=1), preferred_element_type=F32)
            )
        for i in range(4):
            for e in range(2):
                j = (4 * k + i) * 2 + e
                spectra[pl.ds(j * PITCH, SIDE), :] = results[i][:, e * half : (e + 1) * half] * scale
        return 0

    lax.fori_loop(0, SIDE // 8, analyse_first, 0)

    def unsort(k, _):
        results = []
        for e in range(4):
            b = 4 * k + e
            pick = row_j == place_ref[pl.ds(b, 1), :]
            table = jnp.where(pick, 1.0, 0.0)[:, :SIDE].astype(BF16)
            values = jnp.concatenate(
                [
                    spectra[pl.ds(c * BLOCKS + b, SIDE, stride=PITCH), :].astype(BF16)
                    for c in range(2)
                ],
                axis=1,
            )
            results.append(
                lax.dot_general(
                    table, values, (((0,), (0,)), ((), ())), preferred_element_type=F32
                )
            )
        for e in range(4):
            for h in range(2):
                at = pl.ds(2 * (4 * k + e) + h, owners, stride=PITCH)
                back_re[at, :] = results[e][h * owners : (h + 1) * owners, :half]
                back_im[at, :] = results[e][h * owners : (h + 1) * owners, half:]
        return 0

    lax.fori_loop(0, BLOCKS // 4, unsort, 0)

    def store(a, low, values):
        out_ref[a, :, low : low + half] = values

    narrow(back_re, back_im, PITCH, store)


MESH_IDS = pl.DeviceIdType.MESH
CHIPS = 64
BATCH = 8
SPAN = 16


def partners(t, sign=1):
    row, ma = lax.axis_index("row"), lax.axis_index("ma")
    x0, z0 = lax.rem(lax.div(ma, 4), 4), lax.rem(ma, 4)
    y0 = lax.div(ma, 16) * 2 + lax.div(row, 2)
    at_x = [lax.rem(x0 + sign * (t + c) + 8, 4) * 4 for c in range(4)]
    at_z = [lax.rem(z0 + sign * c + 4, 4) for c in range(4)]
    at_y = [lax.rem(y0 + sign * c + 4, 4) for c in range(4)]
    low = [lax.rem(y, 2) for y in at_y]
    high = [lax.div(y, 2) * 16 for y in at_y]
    found = []
    for j in range(SPAN):
        dy = j % 4
        dz = (j // 4 + dy) % 4
        found.append((low[dy], high[dy] + at_x[(dy + dz) % 4] + at_z[dz]))
    return found


def each_partner(action):
    def step(t, _):
        for j, (y_lo, owner) in enumerate(partners(t)):
            run = lambda: action(t * SPAN + j, y_lo, owner, j)
            pl.when(t > 0)(run) if j == 0 else run()
        return 0

    lax.fori_loop(0, CHIPS // SPAN, step, 0)


def greet():
    row, ma = lax.axis_index("row"), lax.axis_index("ma")
    core = lax.rem(row, 2)
    barrier = pltpu.get_barrier_semaphore()
    sibling = (row + 1 - 2 * core, ma)
    pl.semaphore_signal(barrier, inc=1, device_id=sibling, device_id_type=MESH_IDS)

    def signal(i, y_lo, owner, j):
        pl.semaphore_signal(
            barrier, inc=1, device_id=(y_lo * 2 + core, owner), device_id_type=MESH_IDS
        )

    each_partner(signal)
    return lax.div(row, 2), core, ma, sibling


def gathered():
    pl.semaphore_wait(pltpu.get_barrier_semaphore(), CHIPS)


def wait_for(ref, semaphore):
    pltpu.make_async_copy(ref, ref, semaphore).wait()


def send_to(source, target, send_sem, recv_sem, device):
    pltpu.make_async_remote_copy(
        src_ref=source,
        dst_ref=target,
        send_sem=send_sem,
        recv_sem=recv_sem,
        device_id=device,
        device_id_type=MESH_IDS,
    ).start()


def synth_kernel(
    meta, nodes, coeffs_ref, alpha_ref, beta_ref, leg_hbm, out,
    filters, leg_ref, acc_re, acc_im, sums, other, total, load, pair_send, pair_recv, send, recv,
):
    slots, cycles, degrees = leg_ref.shape
    radii = nodes.shape[0]
    rounds = sums.shape[0]
    loading = pltpu.make_async_copy(leg_hbm, leg_ref, load)
    loading.start()
    y_here, core, ma, sibling = greet()

    def fill(r, _):
        filters[pl.ds(r, 1), :] = alpha_ref[pl.ds(nodes[r], 1), :]
        filters[pl.ds(radii + r, 1), :] = beta_ref[pl.ds(nodes[r], 1), :]
        return 0

    lax.fori_loop(0, radii, fill, 0, unroll=8)
    degree = meta[0] + lax.broadcasted_iota(jnp.int32, (1, degrees), 1)
    loading.wait()

    def compute(h, first, last):
        def step(k, _):
            results = []
            for e in range(GROUP):
                at = k * GROUP + e
                slot = meta[1 + h * ROUND + at]
                live = degree >= meta[1 + slots + h * ROUND + at]
                parts = []
                for c in range(2):
                    row = jnp.where(live, coeffs_ref[c, pl.ds(slot, 1), :], 0.0)
                    parts.append((filters[...] * row).astype(BF16))
                filtered = jnp.concatenate(parts, axis=0)
                results.append(
                    lax.dot_general(
                        leg_ref[slot], filtered, (((1,), (1,)), ((), ())), preferred_element_type=F32
                    )
                )
            for e in range(GROUP):
                at = pl.ds(k * GROUP + e, cycles, stride=ROUND + 1)
                acc_re[at, :] = results[e][:, : 2 * radii]
                acc_im[at, :] = results[e][:, 2 * radii :]
            return 0

        lax.fori_loop(first, last, step, 0)

    def swap(h):
        def store(g, low, values):
            sums[h, g // 2, g % 2, :, low : low + 2 * radii] = values

        narrow(acc_re, acc_im, ROUND + 1, store)
        if h == 0:
            gathered()
        send_to(sums.at[h, :, 1 - core], other.at[h], pair_send.at[h], pair_recv.at[h], sibling)

    def post(h):
        wait_for(other.at[h], pair_recv.at[h])

        def add(k, _):
            piece = pl.ds(k * BATCH, BATCH)
            mine = sums[h, piece, core].astype(F32)
            total[h, piece] = (mine + other[h, piece].astype(F32)).astype(BF16)
            return 0

        lax.fori_loop(0, CHIPS // BATCH, add, 0)
        start = y_here * (slots // 2) + h * ROUND
        target = out.at[ma, pl.ds(pl.multiple_of(start, 16), ROUND)]

        def push(i, y_lo, owner, j):
            send_to(
                total.at[h, owner * 2 + y_lo], target, send.at[h], recv, (y_lo * 2 + core, owner)
            )

        each_partner(push)
        pltpu.make_async_copy(total.at[h, ma * 2 + y_here], target, recv).start()
        wait_for(sums.at[h, :, 0], pair_send.at[h])

    steps = ROUND // GROUP
    compute(0, 0, steps)
    swap(0)
    pl.when(y_here == 1)(lambda: compute(1, 0, steps // 2))
    post(0)

    @pl.when(y_here == 1)
    def _():
        compute(1, steps // 2, steps)
        swap(1)
        post(1)

    for h in range(rounds):
        finish = lambda: wait_for(total.at[h, pl.ds(0, CHIPS - 1)], send.at[h])
        if h < rounds // 2:
            finish()
        else:
            pl.when(y_here == 1)(finish)
    wait_for(out, recv)


def adjoint_kernel(
    meta, nodes, radial, alpha_ref, beta_ref, src, leg_hbm, out_ref,
    filters, weights, leg_ref, landed, in_re, in_im, gradient, load, pair_send, pair_recv, send, recv,
):
    slots, cycles, degrees = leg_ref.shape
    radii = nodes.shape[0]
    rounds = landed.shape[0]
    loading = pltpu.make_async_copy(leg_hbm, leg_ref, load)
    loading.start()
    y_here, core, ma, sibling = greet()
    gathered()

    def if_live(h, side, action):
        if h < rounds // 2:
            action()
        else:
            pl.when(side == 1)(action)

    for h in range(rounds):
        rows = pl.ds(h * ROUND, ROUND)

        def keep():
            pltpu.make_async_copy(src.at[ma, rows], landed.at[h, 0, core], recv.at[h, 0]).start()

        if_live(h, y_here, keep)

        def push(i, y_lo, owner, j):
            send_to(
                src.at[owner, rows],
                landed.at[h, i, core],
                send.at[h],
                recv.at[h, i // BATCH],
                (y_lo * 2 + core, owner),
            )

        if h < rounds // 2:
            each_partner(push)
        else:
            for side in range(2):

                def some(i, y_lo, owner, j):
                    if (j % 4) % 2 == 1 - side:
                        push(i, y_lo, owner, j)

                pl.when(y_here == side)(lambda: each_partner(some))

    def fill(r, _):
        node = nodes[r]
        filters[pl.ds(r, 1), :] = alpha_ref[pl.ds(node, 1), :] * radial[node]
        filters[pl.ds(radii + r, 1), :] = beta_ref[pl.ds(node, 1), :] * (2.0 * radial[node])
        return 0

    lax.fori_loop(0, radii, fill, 0, unroll=8)
    high, low = split(filters[...])
    weights[: 2 * radii, :] = high
    weights[2 * radii :, :] = low
    degree = meta[0] + lax.broadcasted_iota(jnp.int32, (1, degrees), 1)
    gradient[...] = jnp.zeros_like(gradient)
    loading.wait()

    def forward(h, k):
        piece = landed.at[h, pl.ds(k * BATCH, BATCH), core]
        wait_for(piece, recv.at[h, k])
        send_to(piece, piece, pair_send.at[h], pair_recv.at[h], sibling)

    def widen(t, h):
        chips = [owner * 2 + y_lo for y_lo, owner in partners(t, -1)]
        for first in range(0, SPAN, 4):
            for target, low in ((in_re, 0), (in_im, 2 * radii)):
                values = [
                    landed[h, t * SPAN + first + e // 2, e % 2, :, low : low + 2 * radii].astype(F32)
                    for e in range(8)
                ]
                for e in range(8):
                    start = (chips[first + e // 2] * 2 + e % 2) * (ROUND + 1)
                    target[pl.ds(start, ROUND), :] = values[e]

    groups = 4
    share = ROUND // groups
    batches = CHIPS // BATCH // groups

    def process(h):
        wait_for(landed.at[h, :, 0], pair_recv.at[h])
        lax.fori_loop(0, CHIPS // SPAN, lambda t, _: (widen(t, h), 0)[1], 0)

        def step(k, _):
            results = []
            for e in range(share):
                at = k * share + e
                slot = meta[1 + h * ROUND + at]
                live = degree >= meta[1 + slots + h * ROUND + at]
                legendre = leg_ref[slot].astype(F32)
                for c, source in enumerate((in_re, in_im)):
                    values = source[pl.ds(at, cycles, stride=ROUND + 1), :].astype(BF16)
                    values = jnp.concatenate([values, values], axis=1)
                    summed = jnp.dot(values, weights[...], preferred_element_type=F32)
                    row = jnp.sum(summed * legendre, axis=0, keepdims=True)
                    results.append((c, at, jnp.where(live, row, 0.0)))
            for c, at, row in results:
                gradient[c, pl.ds(h * ROUND + at, 1), :] = row
            if h + 1 < rounds:

                def ahead():
                    for e in range(batches):
                        forward(h + 1, k * batches + e)

                if_live(h + 1, y_here, ahead)
            return 0

        lax.fori_loop(0, groups, step, 0)

    lax.fori_loop(0, CHIPS // BATCH, lambda k, _: (forward(0, k), 0)[1], 0)
    for h in range(rounds):
        if_live(h, y_here, lambda: process(h))

    def settle(s, _):
        for c in range(2):
            out_ref[c, pl.ds(s, 1), :] = gradient[c, pl.ds(meta[1 + 2 * slots + s], 1), :]
        return 0

    lax.fori_loop(0, slots, settle, 0, unroll=8)

    for h in range(rounds):

        def sent_pair():
            wait_for(landed.at[h, :, 0], pair_send.at[h])

        if_live(h, y_here, sent_pair)
        if h < rounds // 2:
            wait_for(landed.at[h, pl.ds(0, CHIPS - 1), 0], send.at[h])
        else:
            for side in range(2):
                count = CHIPS // 2 - side

                @pl.when(y_here == side)
                def _():
                    wait_for(landed.at[h, pl.ds(0, count), 0], send.at[h])


VMEM = pl.BlockSpec(memory_space=pltpu.VMEM)
SMEM = pl.BlockSpec(memory_space=pltpu.SMEM)
ANY = pl.BlockSpec(memory_space=pl.ANY)


def params(mib):
    return pltpu.CompilerParams(vmem_limit_bytes=mib * 2**20)


def remote_params(collective_id):
    return pltpu.CompilerParams(
        collective_id=collective_id, has_side_effects=True, vmem_limit_bytes=60 * 2**20
    )


def body(
    coeffs, legendre, alpha_table, beta_table, radial_weight, radius_index, orders, cycle_offset, cycle_weight
):
    row_id = lax.axis_index("row")
    ma_id = lax.axis_index("ma")
    ma_count = lax.axis_size("ma")
    slots, cycles, degrees = legendre.shape
    radii = radius_index.shape[0]
    width = 4 * radii
    my_orders = lax.dynamic_slice_in_dim(orders, ma_id * slots, slots)
    where = place(my_orders)
    onehot = where[:, None] == jnp.arange(slots, dtype=jnp.int32)[None, :]
    slot_of = jnp.sum(jnp.where(onehot, jnp.arange(slots, dtype=jnp.int32)[:, None], 0), axis=0)
    order_of = jnp.sum(jnp.where(onehot, my_orders[:, None], 0), axis=0)
    meta = jnp.concatenate([jnp.full((1,), row_id * degrees, jnp.int32), slot_of, order_of, where])
    own = (row_id,)
    offset = lax.dynamic_slice(cycle_offset, own, (1,))
    weight = lax.dynamic_slice(cycle_weight, own, (1,))

    of_owner = orders.reshape(ma_count, 1, slots)
    where = place(of_owner) == jnp.arange(slots, dtype=jnp.int32)[None, :, None]
    placed = jnp.sum(jnp.where(where, lax.bitwise_and(of_owner, SIDE - 1), 0), axis=2)
    placed = jnp.transpose(placed.reshape(ma_count, BLOCKS, 2), (1, 2, 0)).reshape(BLOCKS, SIDE)
    placed = jnp.concatenate([placed, placed], axis=1)

    chips = cycles // 2
    batches = chips // BATCH
    rounds = slots // ROUND
    wide = lambda rows: pltpu.VMEM((cycles * (rows + 1), 2 * radii), F32)
    dma = pltpu.SemaphoreType.DMA
    parts = pl.pallas_call(
        synth_kernel,
        out_shape=jax.ShapeDtypeStruct((ma_count, slots + slots // 2, width), BF16),
        in_specs=[SMEM, SMEM, VMEM, VMEM, VMEM, ANY],
        out_specs=VMEM,
        scratch_shapes=[
            pltpu.VMEM((2 * radii, degrees), F32),
            pltpu.VMEM((slots, cycles, degrees), BF16),
            wide(ROUND),
            wide(ROUND),
            pltpu.VMEM((rounds, chips, 2, ROUND, width), BF16),
            pltpu.VMEM((rounds, chips, ROUND, width), BF16),
            pltpu.VMEM((rounds, chips, ROUND, width), BF16),
            dma,
            dma((rounds,)),
            dma((rounds,)),
            dma((rounds,)),
            dma,
        ],
        compiler_params=remote_params(1),
        name="synth",
    )(meta, radius_index, coeffs, alpha_table, beta_table, legendre)

    tables = [jnp.asarray(table) for table in dft_tables()]
    whole = lambda *shape: pl.BlockSpec(shape, lambda i, off: (0,) * len(shape))
    chosen = lambda table: pl.BlockSpec(
        (1,) + table.shape[1:], lambda i, off: (off[0],) + (0,) * (table.ndim - 1)
    )
    plane = lambda groups: pltpu.VMEM((groups * PITCH, 2 * radii), F32)
    analysed = pl.pallas_call(
        cycle_kernel,
        out_shape=jax.ShapeDtypeStruct((ma_count, slots, width), BF16),
        grid_spec=pltpu.PrefetchScalarGridSpec(
            num_scalar_prefetch=1,
            grid=(1,),
            in_specs=[
                whole(*parts.shape),
                whole(*placed.shape),
                pl.BlockSpec(memory_space=pltpu.SMEM),
                *[chosen(table) for table in tables],
            ],
            out_specs=whole(ma_count, slots, width),
            scratch_shapes=[
                plane(ma_count),
                plane(ma_count),
                plane(SIDE),
                plane(2 * SIDE),
                pltpu.VMEM((SIDE, SIDE, 2 * radii), F32),
                plane(2 * SIDE),
                plane(ma_count),
                plane(ma_count),
            ],
        ),
        compiler_params=params(60),
        name="cycle",
    )(offset, parts, placed, weight, *tables)

    return pl.pallas_call(
        adjoint_kernel,
        out_shape=jax.ShapeDtypeStruct((2, slots, degrees), F32),
        in_specs=[SMEM, SMEM, SMEM, VMEM, VMEM, VMEM, ANY],
        out_specs=VMEM,
        scratch_shapes=[
            pltpu.VMEM((2 * radii, degrees), F32),
            pltpu.VMEM((4 * radii, degrees), BF16),
            pltpu.VMEM((slots, cycles, degrees), BF16),
            pltpu.VMEM((rounds, chips, 2, ROUND, width), BF16),
            wide(ROUND),
            wide(ROUND),
            pltpu.VMEM((2, slots, degrees), F32),
            dma,
            dma((rounds,)),
            dma((rounds,)),
            dma((rounds,)),
            dma((rounds, batches)),
        ],
        compiler_params=remote_params(2),
        name="adjoint",
    )(meta, radius_index, radial_weight, alpha_table, beta_table, analysed, legendre)


def solution(mesh):
    in_specs = (
        P(None, "ma", "row"),
        P("ma", None, "row"),
        P(None, "row"),
        P(None, "row"),
        P(),
        P(),
        P(),
        P("ma"),
        P("ma"),
    )
    return jax.shard_map(
        body, mesh=mesh, in_specs=in_specs, out_specs=P(None, "ma", "row"), check_vma=False
    )
```

time: 132 us -> 114 us (0.86)
  Pallas kernels: 121 us -> 105 us
  local copies, waits for them, and re-layouts: 8.88 us -> 4.52 us
  other arithmetic: 1.93 us -> 3.53 us
    pallas_call x3 -> x1, Pallas kernels: 85.1 us -> 43.2 us  [body(): pl.pallas_call(synth_kernel, out_shape=jax.ShapeDtypeStruct((ma_count, sl...]
    pallas_call x1, Pallas kernels: 13.9 us -> 40.3 us  [body(): pl.pallas_call(adjoint_kernel, out_shape=jax.ShapeDtypeStruct((2, slots,...]
    unnamed x14 -> x1, local copies, waits for them, and re-layouts: 6.5 us -> 1.67 us
    add x1 -> x2, other arithmetic: 0.01 us -> 1.46 us  [place(): return 2 * lax.shift_right_logical(order, 6) + lax.bitwise_and(order, 1)]
where the time goes in v3:
time: 114 us; the launch traced here: 113 us
  Pallas kernels  105 us (92%)
  local copies, waits for them, and re-layouts  4.52 us (4%)
  other arithmetic  3.53 us (3%)
    pallas_call x1, Pallas kernels, body(): pl.pallas_call(synth_kernel, out_shape=jax.ShapeDtypeStruct((ma_count, sl...  43.2 us
    pallas_call x1, Pallas kernels, body(): pl.pallas_call(adjoint_kernel, out_shape=jax.ShapeDtypeStruct((2, slots,...  40.3 us
    pallas_call x1, Pallas kernels, body(): pl.pallas_call(cycle_kernel, out_shape=jax.ShapeDtypeStruct((ma_count, sl...  21.5 us

profile of v3, /device:TPU:15, one launch (start us, length us, event | category | flops | bytes accessed | tf_op | source)
XLA Modules:
  0.0 113.0 jit_solution(8008135726580189438)
XLA Ops:
  0.0 1.2 %dynamic_slice.11.weight_ref = f32[1]{0:T(128)} dynamic-slice(f32[4]{0:T(128)} %param.21, s32[]{:T(128)S(6)} %select_n.21), dynamic_slice_sizes={1} | dynamic-slice | bytes 12 | tf_op jit(solution)/shard_map/dynamic_slice | solution.py:569
  1.2 1.3 %dynamic_slice.10.offset = s32[1]{0:T(128)} dynamic-slice(s32[4]{0:T(128)} %param.20, s32[]{:T(128)S(6)} %select_n.21), dynamic_slice_sizes={1} | dynamic-slice | bytes 12 | tf_op jit(solution)/shard_map/dynamic_slice | solution.py:568
  2.5 0.8 and_add_fusion.1
  3.3 0.1 select_reduce_fusion.2
  3.4 0.7 pad_add_fusion.1.meta
  4.1 0.7 and_add_fusion
  4.8 0.1 add.25
  4.8 0.1 and.40
  4.9 0.6 select_reduce_fusion
  5.5 0.1 copy.15
  5.6 0.1 reshape.44
  5.7 0.7 pad_add_fusion.place_ref
  6.4 43.2 %synth.1.parts_ref = bf16[32,96,256]{2,1,0:T(8,128)(2,1)} custom-call(s32[193]{0:T(256)} %pad_add_fusion.1.meta, s32[64]{0:T(128)} %nodes.3, f32[2,64,512]{2,1,0:T(8,128)} %coeffs_ref.1, f32[64,512]{1,0:T(8,128)} %alpha_ref.3, f32[64,512]{1,0:T(8,128)} %beta_ref.3, bf16[64,128,512]{2,1,0:T(8,128)(2,1)} %leg_hbm.3), custom_call_target="tpu_custom_call" | custom-call | tf_op jit(solution)/shard_map/synth/pallas_call | solution.py:582
  49.6 21.5 %cycle.1.src = bf16[32,64,256]{2,1,0:T(8,128)(2,1)} custom-call(s32[1]{0:T(128)} %dynamic_slice.10.offset, bf16[32,96,256]{2,1,0:T(8,128)(2,1)} %synth.1.parts_ref, s32[32,128]{1,0:T(8,128)} %pad_add_fusion.place_ref, f32[1]{0:T(128)} %dynamic_slice.11.weight_ref, bf16[2,128,192]{2,1,0:T(8,128)(2,1)} %constant.38.clone.first_ref, ...), custom_call_target="tpu_custom_call" | custom-call | tf_op jit(solution)/shard_map/cycle/pallas_call | solution.py:611
  71.1 40.3 %adjoint.1 = f32[2,64,512]{2,1,0:T(8,128)} custom-call(s32[193]{0:T(256)} %pad_add_fusion.1.meta, s32[64]{0:T(128)} %nodes.3, f32[64]{0:T(128)} %radial.1, f32[64,512]{1,0:T(8,128)} %alpha_ref.3, f32[64,512]{1,0:T(8,128)} %beta_ref.3, bf16[32,64,256]{2,1,0:T(8,128)(2,1)} %cycle.1.src, bf16[64,128,512]{2,1,0:T(8,128)(2,1)} %leg_hbm.3), custom_call_target="tpu_custom_call" | custom-call | tf_op jit(solution)/shard_map/adjoint/pallas_call | solution.py:639
  111.4 1.7 %copy.17 = f32[2,64,512]{2,1,0:T(8,128)} copy(f32[2,64,512]{2,1,0:T(8,128)} %adjoint.1) | data formatting | bytes 524288

commit v4 on v3

v4 whole, which is shorter than its diff:
```python
import functools

import jax
import jax.numpy as jnp
import ml_dtypes
import numpy as np
from jax import lax
from jax.experimental import pallas as pl
from jax.experimental.pallas import tpu as pltpu
from jax.sharding import PartitionSpec as P

NPIX = 4096
SIDE = 64
BLOCKS = 32
PITCH = 65
GROUP = 8
ROUND = 32
BF16 = jnp.bfloat16
F32 = jnp.float32


def split_np(table):
    high = table.astype(ml_dtypes.bfloat16)
    low = (table - high.astype(np.float64)).astype(ml_dtypes.bfloat16)
    return high, low


def dft_tables():
    p1 = np.arange(SIDE)
    first, first_t = [], []
    for offset in (0, 1):
        b = np.arange(BLOCKS)
        angle = (np.outer(2 * p1 + offset, b) % 128) * (2.0 * np.pi / 128)
        cos, sin = 2.0 * np.cos(angle), 2.0 * np.sin(angle)
        high, low = split_np(np.block([[cos, -sin], [sin, cos]]))
        first.append(np.concatenate([high, high, low], axis=1))
        first_t.append(np.concatenate([high.T, high.T, low.T], axis=1))
    j = np.arange(SIDE)
    p2 = np.arange(SIDE)
    steps = (p1[:, None] + SIDE * p2[None, :])[:, :, None] * j
    angle = (steps % NPIX) * (2.0 * np.pi / NPIX)
    stage = np.stack([np.cos(angle), -np.sin(angle)], axis=-1).reshape(SIDE, SIDE, 2 * SIDE)
    high, low = split_np(stage)
    second = np.concatenate([high, high, low], axis=2)
    high, low = (np.swapaxes(part, 1, 2) for part in (high, low))
    second_t = np.concatenate([high, high, low], axis=2)
    turn = np.pi * j / NPIX
    turn = np.concatenate([np.cos(turn), np.sin(turn)]).astype(np.float32)
    return turn, np.stack(first), np.stack(first_t), second, second_t


def split(values):
    high = values.astype(BF16)
    low = (values - high.astype(F32)).astype(BF16)
    return high, low


def place(order):
    return 2 * lax.shift_right_logical(order, 6) + lax.bitwise_and(order, 1)


def narrow(in_re, in_im, pitch, store):
    count, half = in_re.shape[0] // pitch, in_re.shape[1]

    def step(k, _):
        for source, low in ((in_re, 0), (in_im, half)):
            values = [
                source[pl.ds((k * GROUP + e) * pitch, pitch - 1), :].astype(BF16)
                for e in range(GROUP)
            ]
            for e in range(GROUP):
                store(k * GROUP + e, low, values[e])
        return 0

    lax.fori_loop(0, count // GROUP, step, 0)


MESH_IDS = pl.DeviceIdType.MESH
CHIPS = 64
BATCH = 8
SPAN = 16


def partners(t, sign=1):
    row, ma = lax.axis_index("row"), lax.axis_index("ma")
    x0, z0 = lax.rem(lax.div(ma, 4), 4), lax.rem(ma, 4)
    y0 = lax.div(ma, 16) * 2 + lax.div(row, 2)
    at_x = [lax.rem(x0 + sign * (t + c) + 8, 4) * 4 for c in range(4)]
    at_z = [lax.rem(z0 + sign * c + 4, 4) for c in range(4)]
    at_y = [lax.rem(y0 + sign * c + 4, 4) for c in range(4)]
    low = [lax.rem(y, 2) for y in at_y]
    high = [lax.div(y, 2) * 16 for y in at_y]
    found = []
    for j in range(SPAN):
        dy = j % 4
        dz = (j // 4 + dy) % 4
        found.append((low[dy], high[dy] + at_x[(dy + dz) % 4] + at_z[dz]))
    return found


def each_partner(action):
    def step(t, _):
        for j, (y_lo, owner) in enumerate(partners(t)):
            run = lambda: action(t * SPAN + j, y_lo, owner, j)
            pl.when(t > 0)(run) if j == 0 else run()
        return 0

    lax.fori_loop(0, CHIPS // SPAN, step, 0)


def greet():
    row, ma = lax.axis_index("row"), lax.axis_index("ma")
    core = lax.rem(row, 2)
    barrier = pltpu.get_barrier_semaphore()
    sibling = (row + 1 - 2 * core, ma)
    pl.semaphore_signal(barrier, inc=1, device_id=sibling, device_id_type=MESH_IDS)

    def signal(i, y_lo, owner, j):
        pl.semaphore_signal(
            barrier, inc=1, device_id=(y_lo * 2 + core, owner), device_id_type=MESH_IDS
        )

    each_partner(signal)
    return lax.div(row, 2), core, ma, sibling


def gathered():
    pl.semaphore_wait(pltpu.get_barrier_semaphore(), CHIPS)


def wait_for(ref, semaphore):
    pltpu.make_async_copy(ref, ref, semaphore).wait()


def send_to(source, target, send_sem, recv_sem, device):
    pltpu.make_async_remote_copy(
        src_ref=source,
        dst_ref=target,
        send_sem=send_sem,
        recv_sem=recv_sem,
        device_id=device,
        device_id_type=MESH_IDS,
    ).start()


def kernel(
    meta, nodes, radial, offsets, cycle_weights, turn, coeffs_ref, alpha_ref, beta_ref, orders_ref,
    first_ref, first_t_ref, second_hbm, second_t_hbm, leg_hbm, out_ref,
    filters, weights, leg_ref, first, first_t, second, second_t, place_ref, acc_re, acc_im, sums, other, total,
    parts_low, parts_high, sum_re, sum_im, spectra, middle, products, analysed, landed, gradient,
    load, load_tables, pair_send, pair_recv, send, recv, pass_send, pass_recv, leave, land,
):
    slots, cycles, degrees = leg_ref.shape
    radii = nodes.shape[0]
    rounds = sums.shape[0]
    loading = pltpu.make_async_copy(leg_hbm, leg_ref, load)
    loading.start()
    tables_loading = [
        pltpu.make_async_copy(second_hbm, second, load_tables.at[0]),
        pltpu.make_async_copy(second_t_hbm, second_t, load_tables.at[1]),
    ]
    y_here, core, ma, sibling = greet()

    def fill(r, _):
        filters[pl.ds(r, 1), :] = alpha_ref[pl.ds(nodes[r], 1), :]
        filters[pl.ds(radii + r, 1), :] = beta_ref[pl.ds(nodes[r], 1), :]
        return 0

    lax.fori_loop(0, radii, fill, 0, unroll=8)
    degree = meta[0] + lax.broadcasted_iota(jnp.int32, (1, degrees), 1)
    loading.wait()
    for part in tables_loading:
        part.start()

    def compute(h, first, last):
        def step(k, _):
            results = []
            for e in range(GROUP):
                at = k * GROUP + e
                slot = meta[1 + h * ROUND + at]
                live = degree >= meta[1 + slots + h * ROUND + at]
                parts = []
                for c in range(2):
                    row = jnp.where(live, coeffs_ref[c, pl.ds(slot, 1), :], 0.0)
                    parts.append((filters[...] * row).astype(BF16))
                filtered = jnp.concatenate(parts, axis=0)
                results.append(
                    lax.dot_general(
                        leg_ref[slot], filtered, (((1,), (1,)), ((), ())), preferred_element_type=F32
                    )
                )
            for e in range(GROUP):
                at = pl.ds(k * GROUP + e, cycles, stride=ROUND + 1)
                acc_re[at, :] = results[e][:, : 2 * radii]
                acc_im[at, :] = results[e][:, 2 * radii :]
            return 0

        lax.fori_loop(first, last, step, 0)

    def swap(h):
        def store(g, low, values):
            sums[h, g // 2, g % 2, :, low : low + 2 * radii] = values

        narrow(acc_re, acc_im, ROUND + 1, store)
        if h == 0:
            gathered()
        send_to(sums.at[h, :, 1 - core], other.at[h], pair_send.at[h], pair_recv.at[h], sibling)

    def post(h):
        wait_for(other.at[h], pair_recv.at[h])

        def add(k, _):
            piece = pl.ds(k * BATCH, BATCH)
            mine = sums[h, piece, core].astype(F32)
            total[h, piece] = (mine + other[h, piece].astype(F32)).astype(BF16)
            return 0

        lax.fori_loop(0, CHIPS // BATCH, add, 0)
        target = parts_low.at[ma, y_here] if h == 0 else parts_high.at[ma]

        def push(i, y_lo, owner, j):
            send_to(
                total.at[h, owner * 2 + y_lo], target, send.at[h], recv.at[h], (y_lo * 2 + core, owner)
            )

        each_partner(push)
        pltpu.make_async_copy(total.at[h, ma * 2 + y_here], target, recv.at[h]).start()
        wait_for(sums.at[h, :, 0], pair_send.at[h])

    steps = ROUND // GROUP
    compute(0, 0, steps)
    swap(0)
    pl.when(y_here == 1)(lambda: compute(1, 0, steps // 2))
    post(0)

    @pl.when(y_here == 1)
    def _():
        compute(1, steps // 2, steps)
        swap(1)
        post(1)

    for part in tables_loading:
        part.wait()

    def refill(r, _):
        node = nodes[r]
        filters[pl.ds(r, 1), :] = alpha_ref[pl.ds(node, 1), :] * radial[node]
        filters[pl.ds(radii + r, 1), :] = beta_ref[pl.ds(node, 1), :] * (2.0 * radial[node])
        return 0

    lax.fori_loop(0, radii, refill, 0, unroll=8)
    high, low = split(filters[...])
    weights[: 2 * radii, :] = high
    weights[2 * radii :, :] = low
    gradient[...] = jnp.zeros_like(gradient)

    own = lax.axis_index("row")
    late = offsets[own].astype(F32)
    for table, chosen in ((first_ref, first), (first_t_ref, first_t)):
        chosen[...] = (
            table[0].astype(F32) * (1.0 - late) + table[1].astype(F32) * late
        ).astype(BF16)

    lane = lax.broadcasted_iota(jnp.int32, orders_ref.shape, 1)
    orders = orders_ref[...]
    place_of = place(orders) - lax.bitwise_and(lax.shift_right_logical(lane, 5), 1)
    inside = lax.bitwise_and(orders, SIDE - 1)

    def locate(b, _):
        found = jnp.where(place_of == 2 * b, inside, 0)
        place_ref[pl.ds(b, 1), :] = jnp.sum(found, axis=0, keepdims=True)
        return 0

    lax.fori_loop(0, BLOCKS, locate, 0, unroll=4)

    owners, half = parts_high.shape[0], 2 * radii

    def gather(h):
        def step(k, _):
            loaded = []
            for e in range(4):
                a = k * 4 + e
                if h == 0:
                    loaded.append(parts_low[a, 0].astype(F32) + parts_low[a, 1].astype(F32))
                else:
                    loaded.append(parts_high[a].astype(F32))
            for e in range(4):
                rows = pl.ds((k * 4 + e) * PITCH + h * ROUND, ROUND)
                sum_re[rows, :] = loaded[e][:, :half]
                sum_im[rows, :] = loaded[e][:, half:]
            return 0

        lax.fori_loop(0, owners // 4, step, 0)

    row_j = lax.broadcasted_iota(jnp.int32, (SIDE, 2 * SIDE), 0)

    def sort(k, _):
        results = []
        for e in range(4):
            b = k * 4 + e
            pick = row_j == place_ref[pl.ds(b, 1), :]
            one = jnp.where((row_j == 0) & (b == 0), 0.5, 1.0)
            table = jnp.where(pick, one, 0.0).astype(BF16)
            terms = []
            for source in (sum_re, sum_im):
                values = jnp.concatenate(
                    [source[pl.ds(2 * b + h, owners, stride=PITCH), :] for h in range(2)], axis=0
                )
                terms.append(jnp.concatenate(split(values), axis=0))
            terms = jnp.concatenate(terms, axis=1)
            results.append((b, jnp.dot(table, terms, preferred_element_type=F32)))
        for b, placed in results:
            spectra[pl.ds(b, SIDE, stride=PITCH), :] = placed[:, :half]
            spectra[pl.ds(BLOCKS + b, SIDE, stride=PITCH), :] = placed[:, half:]
        return 0

    wait_for(parts_low, recv.at[0])
    gather(0)
    lax.fori_loop(0, BLOCKS // 8, sort, 0)
    wait_for(parts_high, recv.at[1])
    gather(1)
    lax.fori_loop(BLOCKS // 8, BLOCKS // 4, sort, 0)

    def synth_first(k, _):
        results = []
        for i in range(4):
            pair = []
            for e in range(2):
                j = (4 * k + i) * 2 + e
                cos, sin = 1.0 + late * (turn[j] - 1.0), late * turn[SIDE + j]
                real = spectra[pl.ds(j * PITCH, BLOCKS), :]
                imag = spectra[pl.ds(j * PITCH + BLOCKS, BLOCKS), :]
                high, low = split(
                    jnp.concatenate([cos * real - sin * imag, sin * real + cos * imag], axis=0)
                )
                pair.append(jnp.concatenate([high, low, high], axis=0))
            results.append(
                jnp.dot(first[...], jnp.concatenate(pair, axis=1), preferred_element_type=F32)
            )
        for i in range(4):
            for e in range(2):
                j = (4 * k + i) * 2 + e
                for c in range(2):
                    middle[pl.ds((2 * j + c) * PITCH, SIDE), :] = results[i][
                        c * SIDE : (c + 1) * SIDE, e * half : (e + 1) * half
                    ]
        return 0

    lax.fori_loop(0, SIDE // 8, synth_first, 0)
    lower = lax.broadcasted_iota(jnp.int32, (SIDE, half), 1) < half // 2

    def synth_second(k, total):
        results = []
        for e in range(4):
            p1 = 4 * k + e
            high, low = split(middle[pl.ds(p1, 2 * SIDE, stride=PITCH), :])
            values = jnp.concatenate([high, low, high], axis=0)
            fields = jnp.dot(second[p1], values, preferred_element_type=F32)
            swapped = pltpu.roll(fields, half // 2, 1)
            product = swapped * jnp.where(lower, swapped, fields)
            total = total + product
            results.append(product)
        for e in range(4):
            products[4 * k + e] = results[e]
        return total

    whole = lax.fori_loop(0, SIDE // 4, synth_second, jnp.zeros((SIDE, half), F32))
    mean = jnp.sum(whole, axis=0, keepdims=True) * (1.0 / NPIX)

    def analyse_second(k, _):
        results = []
        for e in range(4):
            p1 = 4 * k + e
            high, low = split(products[p1] - mean)
            values = jnp.concatenate([high, low, high], axis=0)
            results.append(jnp.dot(second_t[p1], values, preferred_element_type=F32))
        for e in range(4):
            middle[pl.ds(4 * k + e, 2 * SIDE, stride=PITCH), :] = results[e]
        return 0

    lax.fori_loop(0, SIDE // 4, analyse_second, 0)
    scale = cycle_weights[own] * 0.5

    def analyse_first(k, _):
        results = []
        for i in range(4):
            pair = []
            for e in range(2):
                j = (4 * k + i) * 2 + e
                values = jnp.concatenate(
                    [middle[pl.ds((2 * j + c) * PITCH, SIDE), :] for c in range(2)], axis=0
                )
                high, low = split(values)
                pair.append(jnp.concatenate([high, low, high], axis=0))
            results.append(
                jnp.dot(first_t[...], jnp.concatenate(pair, axis=1), preferred_element_type=F32)
            )
        for i in range(4):
            for e in range(2):
                j = (4 * k + i) * 2 + e
                cos = scale + late * (turn[j] * scale - scale)
                sin = late * turn[SIDE + j] * scale
                real = results[i][:BLOCKS, e * half : (e + 1) * half]
                imag = results[i][BLOCKS:, e * half : (e + 1) * half]
                spectra[pl.ds(j * PITCH, BLOCKS), :] = cos * real + sin * imag
                spectra[pl.ds(j * PITCH + BLOCKS, BLOCKS), :] = cos * imag - sin * real
        return 0

    lax.fori_loop(0, SIDE // 8, analyse_first, 0)

    def unsort(k, _):
        results = []
        for e in range(4):
            b = 4 * k + e
            pick = row_j == place_ref[pl.ds(b, 1), :]
            table = jnp.where(pick, 1.0, 0.0)[:, :SIDE].astype(BF16)
            values = jnp.concatenate(
                [
                    spectra[pl.ds(c * BLOCKS + b, SIDE, stride=PITCH), :].astype(BF16)
                    for c in range(2)
                ],
                axis=1,
            )
            results.append(
                lax.dot_general(
                    table, values, (((0,), (0,)), ((), ())), preferred_element_type=F32
                )
            )
        for e in range(4):
            for h in range(2):
                at = pl.ds(2 * (4 * k + e) + h, owners, stride=PITCH)
                sum_re[at, :] = results[e][h * owners : (h + 1) * owners, :half]
                sum_im[at, :] = results[e][h * owners : (h + 1) * owners, half:]
        return 0

    def if_live(h, side, action):
        if h < rounds // 2:
            action()
        else:
            pl.when(side == 1)(action)

    for h in range(rounds):
        lax.fori_loop(h * BLOCKS // 8, (h + 1) * BLOCKS // 8, unsort, 0)

        def pack(k, _):
            for source, low in ((sum_re, 0), (sum_im, half)):
                values = [
                    source[pl.ds((k * GROUP + e) * PITCH + h * ROUND, ROUND), :].astype(BF16)
                    for e in range(GROUP)
                ]
                for e in range(GROUP):
                    analysed[h, k * GROUP + e, :, low : low + half] = values[e]
            return 0

        lax.fori_loop(0, owners // GROUP, pack, 0)

        def keep():
            pltpu.make_async_copy(analysed.at[h, ma], landed.at[h, 0, core], land.at[h, 0]).start()

        if_live(h, y_here, keep)

        def push(i, y_lo, owner, j):
            send_to(
                analysed.at[h, owner],
                landed.at[h, i, core],
                leave.at[h],
                land.at[h, i // BATCH],
                (y_lo * 2 + core, owner),
            )

        if h < rounds // 2:
            each_partner(push)
        else:
            for side in range(2):

                def some(i, y_lo, owner, j):
                    if (j % 4) % 2 == 1 - side:
                        push(i, y_lo, owner, j)

                pl.when(y_here == side)(lambda: each_partner(some))

    def forward(h, k):
        piece = landed.at[h, pl.ds(k * BATCH, BATCH), core]
        wait_for(piece, land.at[h, k])
        send_to(piece, piece, pass_send.at[h], pass_recv.at[h], sibling)

    def widen(t, h):
        chips = [owner * 2 + y_lo for y_lo, owner in partners(t, -1)]
        for first in range(0, SPAN, 4):
            for target, low in ((acc_re, 0), (acc_im, 2 * radii)):
                values = [
                    landed[h, t * SPAN + first + e // 2, e % 2, :, low : low + 2 * radii].astype(F32)
                    for e in range(8)
                ]
                for e in range(8):
                    start = (chips[first + e // 2] * 2 + e % 2) * (ROUND + 1)
                    target[pl.ds(start, ROUND), :] = values[e]

    groups = 4
    share = ROUND // groups
    batches = CHIPS // BATCH // groups

    def process(h):
        wait_for(landed.at[h, :, 0], pass_recv.at[h])
        lax.fori_loop(0, CHIPS // SPAN, lambda t, _: (widen(t, h), 0)[1], 0)

        def step(k, _):
            results = []
            for e in range(share):
                at = k * share + e
                slot = meta[1 + h * ROUND + at]
                live = degree >= meta[1 + slots + h * ROUND + at]
                legendre = leg_ref[slot].astype(F32)
                for c, source in enumerate((acc_re, acc_im)):
                    values = source[pl.ds(at, cycles, stride=ROUND + 1), :].astype(BF16)
                    values = jnp.concatenate([values, values], axis=1)
                    summed = jnp.dot(values, weights[...], preferred_element_type=F32)
                    row = jnp.sum(summed * legendre, axis=0, keepdims=True)
                    results.append((c, at, jnp.where(live, row, 0.0)))
            for c, at, row in results:
                gradient[c, pl.ds(h * ROUND + at, 1), :] = row
            if h + 1 < rounds:

                def ahead():
                    for e in range(batches):
                        forward(h + 1, k * batches + e)

                if_live(h + 1, y_here, ahead)
            return 0

        lax.fori_loop(0, groups, step, 0)

    lax.fori_loop(0, CHIPS // BATCH, lambda k, _: (forward(0, k), 0)[1], 0)
    for h in range(rounds):
        if_live(h, y_here, lambda: process(h))

    def settle(s, _):
        for c in range(2):
            out_ref[c, pl.ds(s, 1), :] = gradient[c, pl.ds(meta[1 + 2 * slots + s], 1), :]
        return 0

    lax.fori_loop(0, slots, settle, 0, unroll=8)

    for h in range(rounds):

        def sent_pair():
            wait_for(landed.at[h, :, 0], pass_send.at[h])

        if_live(h, y_here, sent_pair)
        if h < rounds // 2:
            wait_for(landed.at[h, pl.ds(0, CHIPS - 1), 0], leave.at[h])
        else:
            for side in range(2):
                count = CHIPS // 2 - side

                @pl.when(y_here == side)
                def _():
                    wait_for(landed.at[h, pl.ds(0, count), 0], leave.at[h])

        if_live(h, y_here, lambda: wait_for(total.at[h, pl.ds(0, CHIPS - 1)], send.at[h]))


VMEM = pl.BlockSpec(memory_space=pltpu.VMEM)
SMEM = pl.BlockSpec(memory_space=pltpu.SMEM)
ANY = pl.BlockSpec(memory_space=pl.ANY)


def body(
    coeffs, legendre, alpha_table, beta_table, radial_weight, radius_index, orders, cycle_offset, cycle_weight
):
    row_id = lax.axis_index("row")
    ma_id = lax.axis_index("ma")
    ma_count = lax.axis_size("ma")
    slots, cycles, degrees = legendre.shape
    radii = radius_index.shape[0]
    width = 4 * radii
    my_orders = lax.dynamic_slice_in_dim(orders, ma_id * slots, slots)
    where = place(my_orders)
    onehot = where[:, None] == jnp.arange(slots, dtype=jnp.int32)[None, :]
    slot_of = jnp.sum(jnp.where(onehot, jnp.arange(slots, dtype=jnp.int32)[:, None], 0), axis=0)
    order_of = jnp.sum(jnp.where(onehot, my_orders[:, None], 0), axis=0)
    meta = jnp.concatenate([jnp.full((1,), row_id * degrees, jnp.int32), slot_of, order_of, where])
    orders_t = jnp.tile(jnp.transpose(orders.reshape(ma_count, slots)), (1, 128 // ma_count))
    chips = cycles // 2
    batches = chips // BATCH
    rounds = slots // ROUND
    wide = pltpu.VMEM((cycles * (ROUND + 1), 2 * radii), F32)
    plane = lambda groups: pltpu.VMEM((groups * PITCH, 2 * radii), F32)
    dma = pltpu.SemaphoreType.DMA
    turn, first, first_t, second, second_t = (jnp.asarray(table) for table in dft_tables())
    return pl.pallas_call(
        kernel,
        out_shape=jax.ShapeDtypeStruct((2, slots, degrees), F32),
        in_specs=[SMEM] * 6 + [VMEM] * 6 + [ANY] * 3,
        out_specs=VMEM,
        scratch_shapes=[
            pltpu.VMEM((2 * radii, degrees), F32),
            pltpu.VMEM((4 * radii, degrees), BF16),
            pltpu.VMEM((slots, cycles, degrees), BF16),
            pltpu.VMEM(first.shape[1:], BF16),
            pltpu.VMEM(first_t.shape[1:], BF16),
            pltpu.VMEM(second.shape, BF16),
            pltpu.VMEM(second_t.shape, BF16),
            pltpu.VMEM((BLOCKS, 2 * SIDE), jnp.int32),
            wide,
            wide,
            pltpu.VMEM((rounds, chips, 2, ROUND, width), BF16),
            pltpu.VMEM((rounds, chips, ROUND, width), BF16),
            pltpu.VMEM((rounds, chips, ROUND, width), BF16),
            pltpu.VMEM((ma_count, 2, ROUND, width), BF16),
            pltpu.VMEM((ma_count, ROUND, width), BF16),
            plane(ma_count),
            plane(ma_count),
            plane(SIDE),
            plane(2 * SIDE),
            pltpu.VMEM((SIDE, SIDE, 2 * radii), F32),
            pltpu.VMEM((rounds, ma_count, ROUND, width), BF16),
            pltpu.VMEM((rounds, chips, 2, ROUND, width), BF16),
            pltpu.VMEM((2, slots, degrees), F32),
            dma,
            dma((2,)),
            dma((rounds,)),
            dma((rounds,)),
            dma((rounds,)),
            dma((rounds,)),
            dma((rounds,)),
            dma((rounds,)),
            dma((rounds,)),
            dma((rounds, batches)),
        ],
        compiler_params=pltpu.CompilerParams(
            collective_id=1, has_side_effects=True, vmem_limit_bytes=60 * 2**20
        ),
        name="estimator",
    )(
        meta, radius_index, radial_weight, cycle_offset, cycle_weight, turn, coeffs, alpha_table, beta_table,
        orders_t, first, first_t, second, second_t, legendre,
    )


def solution(mesh):
    in_specs = (
        P(None, "ma", "row"),
        P("ma", None, "row"),
        P(None, "row"),
        P(None, "row"),
        P(),
        P(),
        P(),
        P("ma"),
        P("ma"),
    )
    return jax.shard_map(
        body, mesh=mesh, in_specs=in_specs, out_specs=P(None, "ma", "row"), check_vma=False
    )
```

time: 114 us -> 95.6 us (0.84)
  Pallas kernels: 105 us -> 89.7 us
  other arithmetic: 3.53 us -> 1.52 us
  local copies, waits for them, and re-layouts: 4.52 us -> 3.14 us
    pallas_call x3 -> x1, Pallas kernels: 105 us -> 89.7 us  [body(): pl.pallas_call(kernel, out_shape=jax.ShapeDtypeStruct((2, slots, degrees)...]
    dynamic_slice x2 -> x0, local copies, waits for them, and re-layouts: 2.54 us -> none  [the longest x1 1.3 us: body(): offset = lax.dynamic_slice(cycle_offset, own, (1,))]
where the time goes in v4:
time: 95.6 us; the launch traced here: 94.4 us
  Pallas kernels  89.7 us (94%)
  local copies, waits for them, and re-layouts  3.14 us (3%)
  other arithmetic  1.52 us (2%)
    pallas_call x1, Pallas kernels, body(): pl.pallas_call(kernel, out_shape=jax.ShapeDtypeStruct((2, slots, degrees)...  89.7 us

profile of v4, /device:TPU:15, one launch (start us, length us, event | category | flops | bytes accessed | tf_op | source)
XLA Modules:
  0.0 94.4 jit_solution(3581764290046071999)
XLA Ops:
  0.0 0.8 and_add_fusion
  0.8 0.1 select_reduce_fusion.1
  0.9 0.7 pad_add_fusion.meta
  1.5 0.8 reshape.9
  2.3 0.7 copy.16.orders_ref
  3.0 89.7 %estimator.1 = f32[2,64,512]{2,1,0:T(8,128)} custom-call(s32[193]{0:T(256)} %pad_add_fusion.meta, s32[64]{0:T(128)} %nodes.1, f32[64]{0:T(128)} %radial.1, s32[4]{0:T(128)} %offsets.1, f32[4]{0:T(128)} %cycle_weights.1, f32[128]{0:T(128)} %constant.33.clone.turn, f32[2,64,512]{2,1,0:T(8,128)} %coeffs_ref.1, f32[64,512]{1,0:T(8,128)} %alpha_ref.1, ...), custom_call_target="tpu_custom_call" | custom-call | tf_op jit(solution)/shard_map/estimator/pallas_call | solution.py:591
  92.7 1.7 %copy.18 = f32[2,64,512]{2,1,0:T(8,128)} copy(f32[2,64,512]{2,1,0:T(8,128)} %estimator.1) | data formatting | bytes 524288
  (1 shorter events, 0.0 us)

commit v5 on v4

--- a/solution.py
+++ b/solution.py
@@ -144,7 +144,7 @@
 
 
 def kernel(
-    meta, nodes, radial, offsets, cycle_weights, turn, coeffs_ref, alpha_ref, beta_ref, orders_ref,
+    slot_of, order_list, nodes, radial, offsets, cycle_weights, turn, coeffs_ref, alpha_ref, beta_ref, orders_ref,
     first_ref, first_t_ref, second_hbm, second_t_hbm, leg_hbm, out_ref,
     filters, weights, leg_ref, first, first_t, second, second_t, place_ref, acc_re, acc_im, sums, other, total,
     parts_low, parts_high, sum_re, sum_im, spectra, middle, products, analysed, landed, gradient,
@@ -167,7 +167,8 @@
         return 0
 
     lax.fori_loop(0, radii, fill, 0, unroll=8)
-    degree = meta[0] + lax.broadcasted_iota(jnp.int32, (1, degrees), 1)
+    first_slot = ma * slots
+    degree = lax.axis_index("row") * degrees + lax.broadcasted_iota(jnp.int32, (1, degrees), 1)
     loading.wait()
     for part in tables_loading:
         part.start()
@@ -177,8 +178,8 @@
             results = []
             for e in range(GROUP):
                 at = k * GROUP + e
-                slot = meta[1 + h * ROUND + at]
-                live = degree >= meta[1 + slots + h * ROUND + at]
+                slot = slot_of[h * ROUND + at]
+                live = degree >= order_list[first_slot + slot]
                 parts = []
                 for c in range(2):
                     row = jnp.where(live, coeffs_ref[c, pl.ds(slot, 1), :], 0.0)
@@ -261,10 +262,11 @@
             table[0].astype(F32) * (1.0 - late) + table[1].astype(F32) * late
         ).astype(BF16)
 
-    lane = lax.broadcasted_iota(jnp.int32, orders_ref.shape, 1)
-    orders = orders_ref[...]
-    place_of = place(orders) - lax.bitwise_and(lax.shift_right_logical(lane, 5), 1)
-    inside = lax.bitwise_and(orders, SIDE - 1)
+    turned = jnp.transpose(orders_ref[...])
+    listed = jnp.concatenate([turned[:slots], turned[slots:]] * 4, axis=1)
+    lane = lax.broadcasted_iota(jnp.int32, listed.shape, 1)
+    place_of = place(listed) - lax.bitwise_and(lax.shift_right_logical(lane, 5), 1)
+    inside = lax.bitwise_and(listed, SIDE - 1)
 
     def locate(b, _):
         found = jnp.where(place_of == 2 * b, inside, 0)
@@ -296,15 +298,20 @@
 
     def sort(k, _):
         results = []
-        for e in range(4):
-            b = k * 4 + e
+        for e in range(8):
+            b = k * 8 + e
             pick = row_j == place_ref[pl.ds(b, 1), :]
             one = jnp.where((row_j == 0) & (b == 0), 0.5, 1.0)
             table = jnp.where(pick, one, 0.0).astype(BF16)
             terms = []
             for source in (sum_re, sum_im):
                 values = jnp.concatenate(
-                    [source[pl.ds(2 * b + h, owners, stride=PITCH), :] for h in range(2)], axis=0
+                    [
+                        source[pl.ds(2 * b + h + odd * PITCH, owners // 2, stride=2 * PITCH), :]
+                        for h in range(2)
+                        for odd in range(2)
+                    ],
+                    axis=0,
                 )
                 terms.append(jnp.concatenate(split(values), axis=0))
             terms = jnp.concatenate(terms, axis=1)
@@ -316,17 +323,17 @@
 
     wait_for(parts_low, recv.at[0])
     gather(0)
-    lax.fori_loop(0, BLOCKS // 8, sort, 0)
+    lax.fori_loop(0, BLOCKS // 16, sort, 0)
     wait_for(parts_high, recv.at[1])
     gather(1)
-    lax.fori_loop(BLOCKS // 8, BLOCKS // 4, sort, 0)
+    lax.fori_loop(BLOCKS // 16, BLOCKS // 8, sort, 0)
 
     def synth_first(k, _):
         results = []
-        for i in range(4):
+        for i in range(8):
             pair = []
             for e in range(2):
-                j = (4 * k + i) * 2 + e
+                j = (8 * k + i) * 2 + e
                 cos, sin = 1.0 + late * (turn[j] - 1.0), late * turn[SIDE + j]
                 real = spectra[pl.ds(j * PITCH, BLOCKS), :]
                 imag = spectra[pl.ds(j * PITCH + BLOCKS, BLOCKS), :]
@@ -337,22 +344,22 @@
             results.append(
                 jnp.dot(first[...], jnp.concatenate(pair, axis=1), preferred_element_type=F32)
             )
-        for i in range(4):
+        for i in range(8):
             for e in range(2):
-                j = (4 * k + i) * 2 + e
+                j = (8 * k + i) * 2 + e
                 for c in range(2):
                     middle[pl.ds((2 * j + c) * PITCH, SIDE), :] = results[i][
                         c * SIDE : (c + 1) * SIDE, e * half : (e + 1) * half
                     ]
         return 0
 
-    lax.fori_loop(0, SIDE // 8, synth_first, 0)
+    lax.fori_loop(0, SIDE // 16, synth_first, 0)
     lower = lax.broadcasted_iota(jnp.int32, (SIDE, half), 1) < half // 2
 
     def synth_second(k, total):
         results = []
-        for e in range(4):
-            p1 = 4 * k + e
+        for e in range(16):
+            p1 = 16 * k + e
             high, low = split(middle[pl.ds(p1, 2 * SIDE, stride=PITCH), :])
             values = jnp.concatenate([high, low, high], axis=0)
             fields = jnp.dot(second[p1], values, preferred_element_type=F32)
@@ -360,33 +367,33 @@
             product = swapped * jnp.where(lower, swapped, fields)
             total = total + product
             results.append(product)
-        for e in range(4):
-            products[4 * k + e] = results[e]
+        for e in range(16):
+            products[16 * k + e] = results[e]
         return total
 
-    whole = lax.fori_loop(0, SIDE // 4, synth_second, jnp.zeros((SIDE, half), F32))
+    whole = lax.fori_loop(0, SIDE // 16, synth_second, jnp.zeros((SIDE, half), F32))
     mean = jnp.sum(whole, axis=0, keepdims=True) * (1.0 / NPIX)
 
     def analyse_second(k, _):
         results = []
-        for e in range(4):
-            p1 = 4 * k + e
+        for e in range(16):
+            p1 = 16 * k + e
             high, low = split(products[p1] - mean)
             values = jnp.concatenate([high, low, high], axis=0)
             results.append(jnp.dot(second_t[p1], values, preferred_element_type=F32))
-        for e in range(4):
-            middle[pl.ds(4 * k + e, 2 * SIDE, stride=PITCH), :] = results[e]
-        return 0
-
-    lax.fori_loop(0, SIDE // 4, analyse_second, 0)
+        for e in range(16):
+            middle[pl.ds(16 * k + e, 2 * SIDE, stride=PITCH), :] = results[e]
+        return 0
+
+    lax.fori_loop(0, SIDE // 16, analyse_second, 0)
     scale = cycle_weights[own] * 0.5
 
     def analyse_first(k, _):
         results = []
-        for i in range(4):
+        for i in range(8):
             pair = []
             for e in range(2):
-                j = (4 * k + i) * 2 + e
+                j = (8 * k + i) * 2 + e
                 values = jnp.concatenate(
                     [middle[pl.ds((2 * j + c) * PITCH, SIDE), :] for c in range(2)], axis=0
                 )
@@ -395,9 +402,9 @@
             results.append(
                 jnp.dot(first_t[...], jnp.concatenate(pair, axis=1), preferred_element_type=F32)
             )
-        for i in range(4):
+        for i in range(8):
             for e in range(2):
-                j = (4 * k + i) * 2 + e
+                j = (8 * k + i) * 2 + e
                 cos = scale + late * (turn[j] * scale - scale)
                 sin = late * turn[SIDE + j] * scale
                 real = results[i][:BLOCKS, e * half : (e + 1) * half]
@@ -406,12 +413,12 @@
                 spectra[pl.ds(j * PITCH + BLOCKS, BLOCKS), :] = cos * imag - sin * real
         return 0
 
-    lax.fori_loop(0, SIDE // 8, analyse_first, 0)
+    lax.fori_loop(0, SIDE // 16, analyse_first, 0)
 
     def unsort(k, _):
         results = []
-        for e in range(4):
-            b = 4 * k + e
+        for e in range(8):
+            b = 8 * k + e
             pick = row_j == place_ref[pl.ds(b, 1), :]
             table = jnp.where(pick, 1.0, 0.0)[:, :SIDE].astype(BF16)
             values = jnp.concatenate(
@@ -426,11 +433,13 @@
                     table, values, (((0,), (0,)), ((), ())), preferred_element_type=F32
                 )
             )
-        for e in range(4):
-            for h in range(2):
-                at = pl.ds(2 * (4 * k + e) + h, owners, stride=PITCH)
-                sum_re[at, :] = results[e][h * owners : (h + 1) * owners, :half]
-                sum_im[at, :] = results[e][h * owners : (h + 1) * owners, half:]
+        for e in range(8):
+            for piece in range(4):
+                start = 2 * (8 * k + e) + piece // 2 + piece % 2 * PITCH
+                at = pl.ds(start, owners // 2, stride=2 * PITCH)
+                rows = slice(piece * owners // 2, (piece + 1) * owners // 2)
+                sum_re[at, :] = results[e][rows, :half]
+                sum_im[at, :] = results[e][rows, half:]
         return 0
 
     def if_live(h, side, action):
@@ -440,7 +449,7 @@
             pl.when(side == 1)(action)
 
     for h in range(rounds):
-        lax.fori_loop(h * BLOCKS // 8, (h + 1) * BLOCKS // 8, unsort, 0)
+        lax.fori_loop(h * BLOCKS // 16, (h + 1) * BLOCKS // 16, unsort, 0)
 
         def pack(k, _):
             for source, low in ((sum_re, 0), (sum_im, half)):
@@ -496,7 +505,7 @@
                     start = (chips[first + e // 2] * 2 + e % 2) * (ROUND + 1)
                     target[pl.ds(start, ROUND), :] = values[e]
 
-    groups = 4
+    groups = 2
     share = ROUND // groups
     batches = CHIPS // BATCH // groups
 
@@ -508,14 +517,21 @@
             results = []
             for e in range(share):
                 at = k * share + e
-                slot = meta[1 + h * ROUND + at]
-                live = degree >= meta[1 + slots + h * ROUND + at]
+                slot = slot_of[h * ROUND + at]
+                live = degree >= order_list[first_slot + slot]
                 legendre = leg_ref[slot].astype(F32)
-                for c, source in enumerate((acc_re, acc_im)):
-                    values = source[pl.ds(at, cycles, stride=ROUND + 1), :].astype(BF16)
-                    values = jnp.concatenate([values, values], axis=1)
-                    summed = jnp.dot(values, weights[...], preferred_element_type=F32)
-                    row = jnp.sum(summed * legendre, axis=0, keepdims=True)
+                values = jnp.concatenate(
+                    [
+                        source[pl.ds(at, cycles, stride=ROUND + 1), :].astype(BF16)
+                        for source in (acc_re, acc_im)
+                    ],
+                    axis=0,
+                )
+                values = jnp.concatenate([values, values], axis=1)
+                summed = jnp.dot(values, weights[...], preferred_element_type=F32)
+                for c in range(2):
+                    product = summed[c * cycles : (c + 1) * cycles] * legendre
+                    row = jnp.sum(product, axis=0, keepdims=True)
                     results.append((c, at, jnp.where(live, row, 0.0)))
             for c, at, row in results:
                 gradient[c, pl.ds(h * ROUND + at, 1), :] = row
@@ -536,7 +552,7 @@
 
     def settle(s, _):
         for c in range(2):
-            out_ref[c, pl.ds(s, 1), :] = gradient[c, pl.ds(meta[1 + 2 * slots + s], 1), :]
+            out_ref[c, pl.ds(s, 1), :] = gradient[c, pl.ds(place(order_list[first_slot + s]), 1), :]
         return 0
 
     lax.fori_loop(0, slots, settle, 0, unroll=8)
@@ -575,12 +591,8 @@
     radii = radius_index.shape[0]
     width = 4 * radii
     my_orders = lax.dynamic_slice_in_dim(orders, ma_id * slots, slots)
-    where = place(my_orders)
-    onehot = where[:, None] == jnp.arange(slots, dtype=jnp.int32)[None, :]
+    onehot = place(my_orders)[:, None] == jnp.arange(slots, dtype=jnp.int32)[None, :]
     slot_of = jnp.sum(jnp.where(onehot, jnp.arange(slots, dtype=jnp.int32)[:, None], 0), axis=0)
-    order_of = jnp.sum(jnp.where(onehot, my_orders[:, None], 0), axis=0)
-    meta = jnp.concatenate([jnp.full((1,), row_id * degrees, jnp.int32), slot_of, order_of, where])
-    orders_t = jnp.tile(jnp.transpose(orders.reshape(ma_count, slots)), (1, 128 // ma_count))
     chips = cycles // 2
     batches = chips // BATCH
     rounds = slots // ROUND
@@ -591,7 +603,7 @@
     return pl.pallas_call(
         kernel,
         out_shape=jax.ShapeDtypeStruct((2, slots, degrees), F32),
-        in_specs=[SMEM] * 6 + [VMEM] * 6 + [ANY] * 3,
+        in_specs=[SMEM] * 7 + [VMEM] * 6 + [ANY] * 3,
         out_specs=VMEM,
         scratch_shapes=[
             pltpu.VMEM((2 * radii, degrees), F32),
@@ -633,8 +645,8 @@
         ),
         name="estimator",
     )(
-        meta, radius_index, radial_weight, cycle_offset, cycle_weight, turn, coeffs, alpha_table, beta_table,
-        orders_t, first, first_t, second, second_t, legendre,
+        slot_of, orders, radius_index, radial_weight, cycle_offset, cycle_weight, turn, coeffs, alpha_table, beta_table,
+        orders.reshape(-1, 2 * slots), first, first_t, second, second_t, legendre,
     )
 
 

time: 95.6 us -> 87.2 us (0.912)
  Pallas kernels: 89.7 us -> 83.2 us
  local copies, waits for them, and re-layouts: 3.14 us -> 1.67 us
    pallas_call x1, Pallas kernels: 89.7 us -> 83.2 us  [body(): pl.pallas_call(kernel, out_shape=jax.ShapeDtypeStruct((2, slots, degrees)...]
where the time goes in v5:
time: 87.2 us; the launch traced here: 86.2 us
  Pallas kernels  83.2 us (95%)
  local copies, waits for them, and re-layouts  1.67 us (2%)
  other arithmetic  1.37 us (2%)
    pallas_call x1, Pallas kernels, body(): pl.pallas_call(kernel, out_shape=jax.ShapeDtypeStruct((2, slots, degrees)...  83.2 us

profile of v5, /device:TPU:15, one launch (start us, length us, event | category | flops | bytes accessed | tf_op | source)
XLA Modules:
  0.0 86.2 jit_solution(17565253079950414585)
XLA Ops:
  0.0 0.8 and_add_fusion
  0.8 0.6 select_reduce_fusion.slot_of
  1.4 83.2 %estimator.1 = f32[2,64,512]{2,1,0:T(8,128)} custom-call(s32[64]{0:T(128)} %select_reduce_fusion.slot_of, s32[2048]{0:T(1024)} %order_list.1, s32[64]{0:T(128)} %nodes.1, f32[64]{0:T(128)} %radial.1, s32[4]{0:T(128)} %offsets.1, f32[4]{0:T(128)} %cycle_weights.1, f32[128]{0:T(128)} %constant.26.clone.turn, f32[2,64,512]{2,1,0:T(8,128)} %coeffs_ref.1, ...), custom_call_target="tpu_custom_call" | custom-call | tf_op jit(solution)/shard_map/estimator/pallas_call | solution.py:603
  84.6 1.7 %copy.16 = f32[2,64,512]{2,1,0:T(8,128)} copy(f32[2,64,512]{2,1,0:T(8,128)} %estimator.1) | data formatting | bytes 524288

commit v6 on v5

--- a/solution.py
+++ b/solution.py
@@ -330,10 +330,10 @@
 
     def synth_first(k, _):
         results = []
-        for i in range(8):
+        for i in range(16):
             pair = []
             for e in range(2):
-                j = (8 * k + i) * 2 + e
+                j = (16 * k + i) * 2 + e
                 cos, sin = 1.0 + late * (turn[j] - 1.0), late * turn[SIDE + j]
                 real = spectra[pl.ds(j * PITCH, BLOCKS), :]
                 imag = spectra[pl.ds(j * PITCH + BLOCKS, BLOCKS), :]
@@ -344,22 +344,22 @@
             results.append(
                 jnp.dot(first[...], jnp.concatenate(pair, axis=1), preferred_element_type=F32)
             )
-        for i in range(8):
+        for i in range(16):
             for e in range(2):
-                j = (8 * k + i) * 2 + e
+                j = (16 * k + i) * 2 + e
                 for c in range(2):
                     middle[pl.ds((2 * j + c) * PITCH, SIDE), :] = results[i][
                         c * SIDE : (c + 1) * SIDE, e * half : (e + 1) * half
                     ]
         return 0
 
-    lax.fori_loop(0, SIDE // 16, synth_first, 0)
+    lax.fori_loop(0, SIDE // 32, synth_first, 0)
     lower = lax.broadcasted_iota(jnp.int32, (SIDE, half), 1) < half // 2
 
     def synth_second(k, total):
         results = []
-        for e in range(16):
-            p1 = 16 * k + e
+        for e in range(32):
+            p1 = 32 * k + e
             high, low = split(middle[pl.ds(p1, 2 * SIDE, stride=PITCH), :])
             values = jnp.concatenate([high, low, high], axis=0)
             fields = jnp.dot(second[p1], values, preferred_element_type=F32)
@@ -367,33 +367,33 @@
             product = swapped * jnp.where(lower, swapped, fields)
             total = total + product
             results.append(product)
-        for e in range(16):
-            products[16 * k + e] = results[e]
+        for e in range(32):
+            products[32 * k + e] = results[e]
         return total
 
-    whole = lax.fori_loop(0, SIDE // 16, synth_second, jnp.zeros((SIDE, half), F32))
+    whole = lax.fori_loop(0, SIDE // 32, synth_second, jnp.zeros((SIDE, half), F32))
     mean = jnp.sum(whole, axis=0, keepdims=True) * (1.0 / NPIX)
 
     def analyse_second(k, _):
         results = []
-        for e in range(16):
-            p1 = 16 * k + e
+        for e in range(32):
+            p1 = 32 * k + e
             high, low = split(products[p1] - mean)
             values = jnp.concatenate([high, low, high], axis=0)
             results.append(jnp.dot(second_t[p1], values, preferred_element_type=F32))
-        for e in range(16):
-            middle[pl.ds(16 * k + e, 2 * SIDE, stride=PITCH), :] = results[e]
-        return 0
-
-    lax.fori_loop(0, SIDE // 16, analyse_second, 0)
+        for e in range(32):
+            middle[pl.ds(32 * k + e, 2 * SIDE, stride=PITCH), :] = results[e]
+        return 0
+
+    lax.fori_loop(0, SIDE // 32, analyse_second, 0)
     scale = cycle_weights[own] * 0.5
 
     def analyse_first(k, _):
         results = []
-        for i in range(8):
+        for i in range(16):
             pair = []
             for e in range(2):
-                j = (8 * k + i) * 2 + e
+                j = (16 * k + i) * 2 + e
                 values = jnp.concatenate(
                     [middle[pl.ds((2 * j + c) * PITCH, SIDE), :] for c in range(2)], axis=0
                 )
@@ -402,9 +402,9 @@
             results.append(
                 jnp.dot(first_t[...], jnp.concatenate(pair, axis=1), preferred_element_type=F32)
             )
-        for i in range(8):
+        for i in range(16):
             for e in range(2):
-                j = (8 * k + i) * 2 + e
+                j = (16 * k + i) * 2 + e
                 cos = scale + late * (turn[j] * scale - scale)
                 sin = late * turn[SIDE + j] * scale
                 real = results[i][:BLOCKS, e * half : (e + 1) * half]
@@ -413,7 +413,7 @@
                 spectra[pl.ds(j * PITCH + BLOCKS, BLOCKS), :] = cos * imag - sin * real
         return 0
 
-    lax.fori_loop(0, SIDE // 16, analyse_first, 0)
+    lax.fori_loop(0, SIDE // 32, analyse_first, 0)
 
     def unsort(k, _):
         results = []

time: 87.2 us -> 85.9 us (0.985)
  Pallas kernels: 83.2 us -> 81.9 us
    pallas_call x1, Pallas kernels: 83.2 us -> 81.9 us  [body(): pl.pallas_call(kernel, out_shape=jax.ShapeDtypeStruct((2, slots, degrees)...]
where the time goes in v6:
time: 85.9 us; the launch traced here: 84.9 us
  Pallas kernels  81.9 us (95%)
  local copies, waits for them, and re-layouts  1.67 us (2%)
  other arithmetic  1.37 us (2%)
    pallas_call x1, Pallas kernels, body(): pl.pallas_call(kernel, out_shape=jax.ShapeDtypeStruct((2, slots, degrees)...  81.9 us

profile of v6, /device:TPU:15, one launch (start us, length us, event | category | flops | bytes accessed | tf_op | source)
XLA Modules:
  0.0 84.9 jit_solution(14465217065833695118)
XLA Ops:
  0.0 0.8 and_add_fusion
  0.8 0.6 select_reduce_fusion.slot_of
  1.4 81.9 %estimator.1 = f32[2,64,512]{2,1,0:T(8,128)} custom-call(s32[64]{0:T(128)} %select_reduce_fusion.slot_of, s32[2048]{0:T(1024)} %order_list.1, s32[64]{0:T(128)} %nodes.1, f32[64]{0:T(128)} %radial.1, s32[4]{0:T(128)} %offsets.1, f32[4]{0:T(128)} %cycle_weights.1, f32[128]{0:T(128)} %constant.26.clone.turn, f32[2,64,512]{2,1,0:T(8,128)} %coeffs_ref.1, ...), custom_call_target="tpu_custom_call" | custom-call | tf_op jit(solution)/shard_map/estimator/pallas_call | solution.py:603
  83.2 1.7 %copy.16 = f32[2,64,512]{2,1,0:T(8,128)} copy(f32[2,64,512]{2,1,0:T(8,128)} %estimator.1) | data formatting | bytes 524288
